TPU v7x, 256 devices: a whole 4x4x8 slice. The times are simulated.
256 devices in a mesh: section: 8 (over y, core), tok: 32 (over z, x).
Axes of the slice: x: 4, y: 4, z: 8, core: 2. Of those that a mesh axis runs over, the one named last changes fastest.
Arguments:
- patches: bfloat16 [4096, 6144], P('tok'), may hold values from -6 to 6
- patch_ids: int32 [4096], P('tok'), may hold values from 0 to 255
- pos_table: bfloat16 [256, 6144], replicated, may hold values from -5 to 5
- token_counts: int32 [32], P('tok'), may hold values from 16 to 128, as said below
- norm_gain: float32 [8, 6144], P('section'), may hold values from 0.25 to 1.75
- norm_bias: float32 [8, 6144], P('section'), may hold values from -3 to 3
- branch_scale: float32 [8, 6144], P('section'), may hold values from 0.5 to 2
- act_range: float32 [8, 6144], P('section'), may hold values from 1 to 8
- weight_range: float32 [8, 6144], P('section'), may hold values from 0.125 to 1
- alpha_index: int32 [8], P('section'), may hold values from 2 to 7
Outputs:
- covariance: float32 [8, 128, 6144], P('section')
- channel_mean: float32 [8, 6144], P('section')
Inputs may be any that keep to these rules, and one draw needn't show every extreme that they name: Each shard's calibration tokens are its first token_counts slots; at least one shard is full in every draw.
All inputs are finite; a program needn't handle non-finite values.
Results may differ from a plain program's by a relative error of at most 0.0067.
Values may be sent and summed in bfloat16 or wider, within the bound.
A program may use at most 256 MiB of HBM per device.

v0:
```python
import jax
import jax.numpy as jnp
from jax import lax
from jax.sharding import PartitionSpec as P

BLOCK = 128
MICRO = 4


def from_behind(block, axis, distance):
    devices = range(lax.axis_size(axis))
    route = [(i - distance, i) for i in devices if i - distance in devices]
    return lax.ppermute(block, axis, route)


def combined_all(shard, axis, combine):
    everything = jax.tree.map(lambda part: lax.all_gather(part, axis), shard)
    leading = jax.tree.map(lambda part: part[0], everything)

    def hop(k, so_far):
        return combine(so_far, jax.tree.map(lambda part: part[k], everything))

    return lax.fori_loop(1, lax.axis_size(axis), hop, leading)


def layer_norm(values, gain, bias_row):
    centre = jnp.mean(values, axis=-1, keepdims=True)
    spread = jnp.mean(jnp.square(values - centre), axis=-1, keepdims=True)
    return (values - centre) * lax.rsqrt(spread + 1e-06) * gain + bias_row


def smoothing(act_row, weight_row, alpha_code):
    exponent = alpha_code.astype(jnp.float32) / 8.0
    return jnp.exp(exponent * jnp.log(act_row) + (exponent - 1.0) * jnp.log(weight_row))


def combine_moments(first, second):
    first_count, first_mean, first_gram = first
    second_count, second_mean, second_gram = second
    joined = first_count + second_count
    offset = second_mean - first_mean
    joint_mean = first_mean + offset * (second_count / joined)
    pair_weight = first_count * second_count / joined
    joint_gram = (
        first_gram + second_gram + pair_weight * (offset[:BLOCK][:, None] * offset[None, :])
    )
    return (joined, joint_mean, joint_gram)


def body(
    patches,
    patch_ids,
    pos_table,
    token_counts,
    norm_gain,
    norm_bias,
    branch_scale,
    act_range,
    weight_range,
    alpha_index,
):
    sections = lax.axis_size("section")
    section_index = lax.axis_index("section")
    rows_here = patches.shape[0]
    width = patches.shape[1]
    micro_rows = rows_here // MICRO
    looked_up = jnp.take(pos_table, patch_ids, axis=0).astype(jnp.float32)
    start_rows = (patches.astype(jnp.float32) + looked_up).astype(jnp.bfloat16)
    positions = jnp.arange(rows_here, dtype=jnp.int32)
    valid_flat = (positions < token_counts[0]).astype(jnp.float32)
    factor = smoothing(act_range[0], weight_range[0], alpha_index[0])
    blocks = start_rows.reshape(MICRO, micro_rows, width)
    valid_rows = valid_flat.reshape(MICRO, micro_rows)

    def tick_step(tick, carry):
        incoming, stash = carry
        micro_index = tick - section_index
        active = jnp.logical_and(micro_index >= 0, micro_index < MICRO)
        safe_index = jnp.clip(micro_index, 0, MICRO - 1)
        own_block = lax.dynamic_index_in_dim(blocks, safe_index, 0, keepdims=False)
        current = jnp.where(section_index == 0, own_block, incoming)
        normed = layer_norm(current.astype(jnp.float32), norm_gain[0], norm_bias[0])
        smoothed = (normed / factor).astype(jnp.bfloat16)
        weight_mask = lax.dynamic_index_in_dim(valid_rows, safe_index, 0, keepdims=False).astype(
            jnp.bfloat16
        )
        masked = smoothed * weight_mask[:, None]
        previous = lax.dynamic_index_in_dim(stash, safe_index, 0, keepdims=False)
        kept = jnp.where(active, masked, previous)
        stash = lax.dynamic_update_index_in_dim(stash, kept, safe_index, 0)
        updated = (current.astype(jnp.float32) + branch_scale[0] * jax.nn.gelu(normed)).astype(
            jnp.bfloat16
        )
        passed = from_behind(updated, "section", 1)
        return (passed, stash)

    initial = (
        jnp.zeros((micro_rows, width), jnp.bfloat16),
        jnp.zeros((MICRO, micro_rows, width), jnp.bfloat16),
    )
    carried = lax.fori_loop(0, sections + MICRO - 1, tick_step, initial)
    masked = carried[1].reshape(rows_here, width)
    ones_row = jnp.ones((1, rows_here), jnp.bfloat16)
    sum_first = jnp.dot(ones_row, masked, preferred_element_type=jnp.float32)[0]
    sum_second = lax.dot_general(
        masked[:, :BLOCK], masked, (((0,), (0,)), ((), ())), preferred_element_type=jnp.float32
    )
    own_count = token_counts.astype(jnp.float32)
    local_mean = sum_first / own_count
    local_gram = sum_second - own_count * (local_mean[:BLOCK][:, None] * local_mean[None, :])
    total_count, mean_row, gram_block = combined_all(
        (own_count, local_mean, local_gram), "tok", combine_moments
    )
    return ((gram_block / total_count)[None], mean_row[None])


def solution(mesh):
    in_specs = (
        P("tok", None),
        P("tok"),
        P(),
        P("tok"),
        P("section", None),
        P("section", None),
        P("section", None),
        P("section", None),
        P("section", None),
        P("section"),
    )
    out_specs = (P("section", None, None), P("section", None))
    return jax.shard_map(body, mesh=mesh, in_specs=in_specs, out_specs=out_specs, check_vma=False)
```

profile of v0, /device:TPU:1, one launch (start us, length us, event | category | flops | bytes accessed | tf_op | source)
XLA Modules:
  0.0 1089.2 jit_solution(7325292649571802104)
XLA Ops:
  19.2 144.2 %while.35 = (s32[]{:T(128)}, bf16[32,6144]{1,0:T(8,128)(2,1)}, bf16[4,32,6144]{2,1,0:T(8,128)(2,1)}, pred[]{:T(512)}, s32[]{:T(128)}, /*index=5*/bf16[4,32,6144]...) while((s32[]{:T(128)}, bf16[32,6144]{1,0:T(8,128)(2,1)}, ...), condition=%wide.region_3.4_spmd, body=%wide.region_0.3_spmd.sunk | while | flops 6881320 | bytes 6047552 | solution.py:101
  22.9 4.6 collective-permute-start
  36.2 4.4 collective-permute-start
  49.3 4.4 collective-permute-start
  62.3 4.4 collective-permute-start
  75.4 4.4 collective-permute-start
  88.5 4.4 collective-permute-start
  101.6 4.4 collective-permute-start
  114.7 4.4 collective-permute-start
  127.8 4.4 collective-permute-start
  140.9 4.4 collective-permute-start
  154.0 4.4 collective-permute-start
  168.9 44.8 %all-gather.1 = f32[196608]{0:T(1024)S(1)} all-gather(f32[6144]{0:T(1024)S(1)} %broadcast_divide_fusion), channel_id=3, replica_groups=mesh['section'=8,'tok'=32] {'tok'}, dimensions={0}, use_global_device_ids=true | all-gather | bytes 811008 | tf_op jit(solution)/shard_map/all_gather | solution.py:17
  218.2 60.1 %all-reduce = f32[32]{0:T(128)S(1)} all-reduce(f32[32]{0:T(128)S(1)} %convert_dynamic-update-slice_fusion), channel_id=2, replica_groups=mesh['section'=8,'tok'=32] {'tok'}, use_global_device_ids=true, to_apply=%add | all-reduce | flops 32 | bytes 256
  278.3 527.4 %all-gather.5.cloned.1.call-done = f32[4096,6144]{1,0:T(8,128)} async-done(((f32[128,6144]{1,0:T(8,128)}), f32[4096,6144]{1,0:T(8,128)}) %all-gather.5.cloned.1.call-update) | async-done | bytes 100663312 | tf_op jit(solution)/shard_map/all_gather | solution.py:17
  809.6 268.9 %while.36 = (s32[]{:T(128)}, f32[1]{0:T(128)}, f32[6144]{0:T(1024)S(1)}, f32[128,6144]{1,0:T(8,128)}, f32[32,1]{0,1:T(1,128)S(1)}, /*index=5*/f32[32,6144]{1,0:T...) while((s32[]{:T(128)}, f32[1]{0:T(128)}, f32[6144]{0:T(1024)S(1)}, f32[128,6144]{1,0:T(8,128)}, ...), condition=%wide.region_5.6_spmd, body=%wide.region_4.5_spmd.sunk | while | flops 3164169 | bytes 9610963 | solution.py:23
  813.1 5.1 fusion.35
  821.8 5.1 fusion.35
  830.5 5.1 fusion.35
  839.2 5.1 fusion.35
  847.8 5.1 fusion.35
  856.5 5.1 fusion.35
  865.2 5.1 fusion.35
  873.9 5.1 fusion.35
  882.5 5.1 fusion.35
  891.2 5.1 fusion.35
  899.9 5.1 fusion.35
  908.6 5.1 fusion.35
  917.2 5.1 fusion.35
  925.9 5.1 fusion.35
  934.6 5.1 fusion.35
  943.3 5.1 fusion.35
  951.9 5.1 fusion.35
  960.6 5.1 fusion.35
  969.3 5.1 fusion.35
  978.0 5.1 fusion.35
  986.6 5.1 fusion.35
  995.3 5.1 fusion.35
  1004.0 5.1 fusion.35
  1012.7 5.1 fusion.35
  1021.3 5.1 fusion.35
  1030.0 5.1 fusion.35
  1038.7 5.1 fusion.35
  1047.4 5.1 fusion.35
  1056.0 5.1 fusion.35
  1064.7 5.1 fusion.35
  1073.4 5.1 fusion.35
  1078.5 3.9 divide_bitcast_fusion
  (257 shorter events, 169.6 us)
Async XLA Ops:
  7.2 3.0 copy-start
  7.2 798.5 %all-gather.5.cloned.1.call-start = ((), (), s32[]{:S(2)}) async-start(), calls=%async_computation | async-start | bytes 103809024 | tf_op jit(solution)/shard_map/all_gather | solution.py:17
  10.1 2.7 copy-start.3
  10.1 2.6 copy-start.4
  22.9 9.6 collective-permute-start
  36.2 9.4 collective-permute-start
  49.3 9.4 collective-permute-start
  62.3 9.4 collective-permute-start
  75.4 9.4 collective-permute-start
  88.5 9.4 collective-permute-start
  101.6 9.4 collective-permute-start
  114.7 9.4 collective-permute-start
  127.8 9.4 collective-permute-start
  140.9 9.4 collective-permute-start
  154.0 9.4 collective-permute-start
  168.9 47.9 %copy-start.5 = (u32[256]{0:T(256)S(1)}, u32[256]{0:T(256)}, u32[]{:S(2)}) copy-start(u32[256]{0:T(256)} %constant.186) | copy-start | bytes 3076
  213.7 0.9 copy-start.1
  278.3 531.3 %slice-start = ((f32[196608]{0:T(1024)}), f32[6144]{0:T(1024)S(1)}, s32[]{:S(2)}) async-start(f32[196608]{0:T(1024)} %copy-done.1), calls=%async_computation.1 | async-start | bytes 49152 | tf_op jit(solution)/shard_map/slice | solution.py:18
  1078.5 3.9 copy-start.2
Sparse Core Ops, SparseCore 0:
  169.0 636.6 all-gather.4
where the time goes:
time: 1090 us
  waiting for transfers between devices  540 us (50%)
  other arithmetic  233 us (21%)
  blocking collectives  105 us (10%)
  local copies, waits for them, and re-layouts  81.1 us (7%)
  loops' own time  60.9 us (6%)
  starting transfers between devices  48.4 us (4%)
  between operations  15.5 us (1%)
    all_gather x1, waiting for transfers between devices, combined_all(): everything = jax.tree.map(lambda part: lax.all_gather(part, axis), shard)  527 us
    add x31, other arithmetic, combine_moments(): first_gram + second_gram  159 us
    another operation x1, loops' own time, combined_all(): return lax.fori_loop(1, lax.axis_size(axis), hop, leading)  60.6 us
    unnamed x1, blocking collectives  60.1 us
    dynamic_slice x62, local copies, waits for them, and re-layouts, hop(): return combine(so_far, jax.tree.map(lambda part: part[k], everything))  49.2 us
    ppermute x11, starting transfers between devices, from_behind(): return lax.ppermute(block, axis, route)  48.4 us
    all_gather x1, blocking collectives, combined_all(): everything = jax.tree.map(lambda part: lax.all_gather(part, axis), shard)  44.8 us
    dynamic_update_slice x11, other arithmetic, tick_step(): stash = lax.dynamic_update_index_in_dim(stash, kept, safe_index, 0)  22.9 us
  transfers between devices with their start and end apart: 12, of which 12 were waited for; matrix products, arithmetic and copies ran while one was open for 4% of the time, Pallas kernels for 0%

commit v1 on v0

v1 whole, which is shorter than its diff:
```python
import functools

import jax
import jax.numpy as jnp
from jax import lax
from jax.experimental import pallas as pl
from jax.experimental.pallas import tpu as pltpu
from jax.sharding import PartitionSpec as P

BLOCK = 128
RING_X = 4
STEP = 512
F32 = jnp.float32
BF16 = jnp.bfloat16
MESH = pl.DeviceIdType.MESH
CONTRACT_ROWS = (((0,), (0,)), ((), ()))


def columns(c, size=STEP):
    return pl.ds(pl.multiple_of(c * size, size), size)


def fold_lanes(values):
    total = values[:, :128]
    for k in range(1, values.shape[1] // 128):
        total = total + values[:, k * 128:(k + 1) * 128]
    return total


def kernel(
    sections,
    toks,
    ids,
    count,
    alpha,
    patches,
    table,
    gain,
    bias,
    scale,
    act,
    weight,
    out_cov,
    out_mean,
    own_patches,
    table_here,
    ranges,
    params,
    hidden,
    smooth,
    tokens,
    gram,
    mean_send,
    gram_x,
    mean_x,
    part_z,
    mean_z_send,
    gram_z,
    mean_z,
    spread,
    slab,
    full,
    mean_full,
    load_sem,
    par_send,
    par_recv,
    smo_send,
    smo_recv,
    rsx_send,
    rsx_recv,
    rmx_send,
    rmx_recv,
    rsz_send,
    rsz_recv,
    rmz_send,
    rmz_recv,
    agz_send,
    agz_recv,
    agx_send,
    agx_recv,
    agm_send,
    agm_recv,
    store_sem,
):
    s = lax.axis_index("section")
    t = lax.axis_index("tok")
    nx = RING_X
    nz = toks // nx
    x = lax.rem(t, nx)
    z = lax.div(t, nx)
    width = patches.shape[1]
    rows = patches.shape[0] // sections
    wide = width // nx
    slim = BLOCK // nz
    steps = width // STEP

    def to_section(other):
        return {"section": other, "tok": t}

    def to_x(other):
        return {"section": s, "tok": z * nx + other}

    def to_z(other):
        return {"section": s, "tok": other * nx + x}

    def others(size, me, fn):
        def go(k, _):
            fn(lax.rem(me + k, size))
            return 0

        lax.fori_loop(1, size, go, 0)

    loads = [
        pltpu.make_async_copy(act, ranges.at[0], load_sem.at[0]),
        pltpu.make_async_copy(weight, ranges.at[1], load_sem.at[1]),
        pltpu.make_async_copy(gain, params.at[s, 0], load_sem.at[2]),
        pltpu.make_async_copy(bias, params.at[s, 1], load_sem.at[3]),
        pltpu.make_async_copy(scale, params.at[s, 2], load_sem.at[4]),
        pltpu.make_async_copy(
            patches.at[pl.ds(pl.multiple_of(s * rows, rows), rows)], own_patches, load_sem.at[5]
        ),
        pltpu.make_async_copy(table, table_here, load_sem.at[6]),
    ]
    for load in loads:
        load.start()

    barrier = pltpu.get_barrier_semaphore()

    def greet(where):
        pl.semaphore_signal(barrier, inc=1, device_id=where, device_id_type=MESH)

    others(sections, s, lambda k: greet(to_section(k)))
    others(nx, x, lambda k: greet(to_x(k)))
    others(nz, z, lambda k: greet(to_z(k)))

    loads[0].wait()
    loads[1].wait()
    exponent = jnp.full((1, STEP), alpha[0], jnp.int32).astype(F32) / 8.0

    def factor_step(c, _):
        cols = columns(c)
        log_factor = exponent * jnp.log(ranges[0, :, cols]) + (exponent - 1.0) * jnp.log(
            ranges[1, :, cols]
        )
        params[s, 3, :, cols] = jnp.exp(-log_factor)
        return 0

    lax.fori_loop(0, steps, factor_step, 0)
    for load in loads[2:5]:
        load.wait()
    pl.semaphore_wait(barrier, sections - 1 + nx - 1 + nz - 1)

    def params_copy(layer, other):
        return pltpu.make_async_remote_copy(
            src_ref=params.at[layer],
            dst_ref=params.at[layer],
            send_sem=par_send.at[other],
            recv_sem=par_recv.at[layer],
            device_id=to_section(other),
            device_id_type=MESH,
        )

    others(sections, s, lambda k: params_copy(s, k).start())

    loads[5].wait()
    loads[6].wait()
    patch = lax.broadcasted_iota(jnp.int32, (rows, table.shape[0]), 1)
    row = lax.broadcasted_iota(jnp.int32, (rows, table.shape[0]), 0)
    wanted = jnp.zeros((rows, table.shape[0]), jnp.int32)
    for r in range(rows):
        wanted = jnp.where(row == r, ids[s * rows + r], wanted)
    pick = (patch == wanted).astype(F32).astype(BF16)

    def start_step(c, total):
        cols = columns(c)
        looked_up = jnp.dot(pick, table_here[:, cols], preferred_element_type=F32)
        first = (own_patches[:, cols].astype(F32) + looked_up).astype(BF16).astype(F32)
        hidden[:, cols] = first
        return total + fold_lanes(first)

    no_total = jnp.zeros((rows, 128), F32)
    first_total = lax.fori_loop(0, steps, start_step, no_total)

    def smooth_copy(layer, source):
        return pltpu.make_async_remote_copy(
            src_ref=smooth.at[layer],
            dst_ref=tokens.at[source],
            send_sem=smo_send.at[layer],
            recv_sem=smo_recv.at[source],
            device_id=to_section(layer),
            device_id_type=MESH,
        )

    def layer_step(layer, total):
        @pl.when(layer != s)
        def _():
            params_copy(layer, s).wait_recv()

        centre = jnp.sum(total, axis=1, keepdims=True) * (1.0 / width)

        def spread_step(c, squares):
            away = hidden[:, columns(c)] - centre
            return squares + fold_lanes(away * away)

        squares = lax.fori_loop(0, steps, spread_step, no_total)
        variance = jnp.sum(squares, axis=1, keepdims=True) * (1.0 / width)
        inverse = lax.rsqrt(variance + 1e-06)

        def value_step(c, new_total):
            cols = columns(c)
            current = hidden[:, cols]
            normed = (current - centre) * inverse * params[layer, 0, :, cols] + params[
                layer, 1, :, cols
            ]
            smooth[layer, :, cols] = (normed * params[layer, 3, :, cols]).astype(BF16)
            inner = normed * (0.7978845608028654 + 0.035677408136300125 * (normed * normed))
            branch = 0.5 * normed * (1.0 + jnp.tanh(inner))
            updated = (current + params[layer, 2, :, cols] * branch).astype(BF16).astype(F32)
            hidden[:, cols] = updated
            return new_total + fold_lanes(updated)

        new_total = lax.fori_loop(0, steps, value_step, no_total)

        @pl.when(layer != s)
        def _():
            smooth_copy(layer, s).start()

        return new_total

    lax.fori_loop(0, sections, layer_step, first_total)
    tokens[s] = smooth[s]
    others(sections, s, lambda k: smooth_copy(s, k).wait_recv())

    shard_rows = sections * rows
    used = jnp.full((1, 128), count[0], jnp.int32)
    used_f = used.astype(F32)
    position = lax.broadcasted_iota(jnp.int32, (shard_rows, 128), 0)
    valid = (position < count[0]).astype(F32).astype(BF16)
    across = lax.broadcasted_iota(jnp.int32, (16, shard_rows), 1)
    valid_row = (across < count[0]).astype(F32).astype(BF16)
    block = tokens[:, :, :BLOCK].reshape(shard_rows, BLOCK) * valid
    block_sum = lax.dot_general(block, valid, CONTRACT_ROWS, preferred_element_type=F32)
    share = 1.0 / used_f[:, :1]

    def gram_step(c, _):
        cols = columns(c)
        here = tokens[:, :, cols].reshape(shard_rows, STEP)
        mean_here = jnp.dot(valid_row, here, preferred_element_type=F32)[:1] * share
        moments = lax.dot_general(block, here, CONTRACT_ROWS, preferred_element_type=F32)
        gram[:, cols] = (moments - block_sum[:, :1] * mean_here).astype(BF16)
        mean_full[:, cols] = mean_here
        return 0

    lax.fori_loop(0, steps, gram_step, 0)
    for k in range(nx):
        mean_send[k, :, :wide] = mean_full[:, k * wide:(k + 1) * wide]
        mean_send[k, :, wide:wide + BLOCK] = mean_full[:, :BLOCK]
        mean_send[k, :, wide + BLOCK:] = used_f

    def wide_cols(k):
        return pl.ds(pl.multiple_of(k * wide, wide), wide)

    def rsx(target, source):
        return (
            pltpu.make_async_remote_copy(
                src_ref=gram.at[:, wide_cols(target)],
                dst_ref=gram_x.at[source],
                send_sem=rsx_send.at[target],
                recv_sem=rsx_recv.at[source],
                device_id=to_x(target),
                device_id_type=MESH,
            ),
            pltpu.make_async_remote_copy(
                src_ref=mean_send.at[target],
                dst_ref=mean_x.at[source],
                send_sem=rmx_send.at[target],
                recv_sem=rmx_recv.at[source],
                device_id=to_x(target),
                device_id_type=MESH,
            ),
        )

    def start_both(pair):
        pair[0].start()
        pair[1].start()

    def recv_both(pair):
        pair[0].wait_recv()
        pair[1].wait_recv()

    others(nx, x, lambda k: start_both(rsx(k, x)))
    mean_x[x] = mean_send[x]
    others(nx, x, lambda k: recv_both(rsx(x, k)))

    def merge_means(means, size):
        rows_of = [means[k] for k in range(size)]
        counts = [one[:, wide + BLOCK:wide + BLOCK + 1] for one in rows_of]
        joined = functools.reduce(jnp.add, counts)
        middle = functools.reduce(
            jnp.add, [one[:, :wide + BLOCK] * n for one, n in zip(rows_of, counts)]
        ) / joined
        index = lax.broadcasted_iota(jnp.int32, (8, wide + BLOCK), 0)
        away = jnp.zeros((8, wide + BLOCK), F32)
        weight_of = jnp.zeros((8, 1), F32)
        index_one = lax.broadcasted_iota(jnp.int32, (8, 1), 0)
        for k in range(size):
            away = jnp.where(index == k, rows_of[k][:, :wide + BLOCK] - middle, away)
            weight_of = jnp.where(index_one == k, counts[k], weight_of)
        pushed = away[:, wide:] * weight_of
        spread[...] = lax.dot_general(
            pushed, away[:, :wide], CONTRACT_ROWS,
            precision=lax.Precision.HIGHEST, preferred_element_type=F32,
        )
        return joined, middle

    joined_x, middle_x = merge_means(mean_x, nx)
    mean_z_send[:, :wide + BLOCK] = middle_x
    mean_z_send[:, wide + BLOCK:] = jnp.broadcast_to(joined_x, (1, BLOCK))

    def join_x(k, _):
        here = pl.ds(pl.multiple_of(k * slim, slim), slim)
        total = spread[here, :] + gram[here, wide_cols(x)].astype(F32)
        for j in range(1, nx):
            total = total + gram_x[lax.rem(x + j, nx), here, :].astype(F32)
        part_z[k] = total.astype(BF16)
        return 0

    lax.fori_loop(0, nz, join_x, 0)

    def rsz(target, source):
        return (
            pltpu.make_async_remote_copy(
                src_ref=part_z.at[target],
                dst_ref=gram_z.at[source],
                send_sem=rsz_send.at[target],
                recv_sem=rsz_recv.at[source],
                device_id=to_z(target),
                device_id_type=MESH,
            ),
            pltpu.make_async_remote_copy(
                src_ref=mean_z_send,
                dst_ref=mean_z.at[source],
                send_sem=rmz_send.at[target],
                recv_sem=rmz_recv.at[source],
                device_id=to_z(target),
                device_id_type=MESH,
            ),
        )

    others(nz, z, lambda k: start_both(rsz(k, z)))
    mean_z[z] = mean_z_send[...]
    gram_z[z] = part_z[z]
    others(nz, z, lambda k: recv_both(rsz(z, k)))

    joined_z, middle_z = merge_means(mean_z, nz)
    total = spread[pl.ds(pl.multiple_of(z * slim, slim), slim), :]
    for k in range(nz):
        total = total + gram_z[k].astype(F32)
    slab[z] = (total / joined_z).astype(BF16)
    mean_full[:, wide_cols(x)] = middle_z[:, :wide]

    def agz(target, source):
        return pltpu.make_async_remote_copy(
            src_ref=slab.at[source],
            dst_ref=slab.at[source],
            send_sem=agz_send.at[target],
            recv_sem=agz_recv.at[source],
            device_id=to_z(target),
            device_id_type=MESH,
        )

    def agm(target, source):
        return pltpu.make_async_remote_copy(
            src_ref=mean_full.at[:, wide_cols(source)],
            dst_ref=mean_full.at[:, wide_cols(source)],
            send_sem=agm_send.at[target],
            recv_sem=agm_recv.at[source],
            device_id=to_x(target),
            device_id_type=MESH,
        )

    others(nz, z, lambda k: agz(k, z).start())
    others(nx, x, lambda k: agm(k, x).start())
    others(nz, z, lambda k: agz(z, k).wait_recv())

    def agx(target, source):
        return pltpu.make_async_remote_copy(
            src_ref=slab,
            dst_ref=full.at[source],
            send_sem=agx_send.at[target],
            recv_sem=agx_recv.at[source],
            device_id=to_x(target),
            device_id_type=MESH,
        )

    others(nx, x, lambda k: agx(k, x).start())
    full[x] = slab[...]

    def store(source):
        return pltpu.make_async_copy(full.at[source], out_cov.at[source], store_sem.at[source])

    store(x).start()
    others(nx, x, lambda k: agm(x, k).wait_recv())
    mean_store = pltpu.make_async_copy(mean_full, out_mean, store_sem.at[nx])
    mean_store.start()

    def arrived(k):
        agx(x, k).wait_recv()
        store(k).start()

    others(nx, x, arrived)

    others(sections, s, lambda k: params_copy(s, k).wait_send())
    others(sections, s, lambda k: smooth_copy(k, s).wait_send())
    others(nx, x, lambda k: rsx(k, x)[0].wait_send())
    others(nx, x, lambda k: rsx(k, x)[1].wait_send())
    others(nz, z, lambda k: rsz(k, z)[0].wait_send())
    others(nz, z, lambda k: rsz(k, z)[1].wait_send())
    others(nz, z, lambda k: agz(k, z).wait_send())
    others(nx, x, lambda k: agm(k, x).wait_send())
    others(nx, x, lambda k: agx(k, x).wait_send())
    mean_store.wait()
    for k in range(nx):
        store(k).wait()


def body(
    patches, patch_ids, pos_table, token_counts, norm_gain, norm_bias, branch_scale, act_range,
    weight_range, alpha_index,
):
    sections = lax.axis_size("section")
    toks = lax.axis_size("tok")
    nx, nz = RING_X, toks // RING_X
    width = patches.shape[1]
    rows = patches.shape[0] // sections
    wide = width // nx
    slim = BLOCK // nz
    meta = wide + 2 * BLOCK
    dma = pltpu.SemaphoreType.DMA
    smem = pl.BlockSpec(memory_space=pltpu.SMEM)
    hbm = pl.BlockSpec(memory_space=pl.ANY)
    vmem = pltpu.VMEM
    cov, mean = pl.pallas_call(
        functools.partial(kernel, sections, toks),
        out_shape=(
            jax.ShapeDtypeStruct((nx, nz, slim, wide), BF16),
            jax.ShapeDtypeStruct((1, width), F32),
        ),
        in_specs=[smem] * 3 + [hbm] * 7,
        out_specs=(hbm, hbm),
        scratch_shapes=[
            vmem((rows, width), BF16),
            vmem(pos_table.shape, BF16),
            vmem((2, 1, width), F32),
            vmem((sections, 4, 1, width), F32),
            vmem((rows, width), F32),
            vmem((sections, rows, width), BF16),
            vmem((sections, rows, width), BF16),
            vmem((BLOCK, width), BF16),
            vmem((nx, 1, meta), F32),
            vmem((nx, BLOCK, wide), BF16),
            vmem((nx, 1, meta), F32),
            vmem((nz, slim, wide), BF16),
            vmem((1, meta), F32),
            vmem((nz, slim, wide), BF16),
            vmem((nz, 1, meta), F32),
            vmem((BLOCK, wide), F32),
            vmem((nz, slim, wide), BF16),
            vmem((nx, nz, slim, wide), BF16),
            vmem((1, width), F32),
            dma((7,)),
            dma((sections,)),
            dma((sections,)),
            dma((sections,)),
            dma((sections,)),
            dma((nx,)),
            dma((nx,)),
            dma((nx,)),
            dma((nx,)),
            dma((nz,)),
            dma((nz,)),
            dma((nz,)),
            dma((nz,)),
            dma((nz,)),
            dma((nz,)),
            dma((nx,)),
            dma((nx,)),
            dma((nx,)),
            dma((nx,)),
            dma((nx + 1,)),
        ],
        compiler_params=pltpu.CompilerParams(
            collective_id=0, has_side_effects=True, vmem_limit_bytes=40 * 1024 * 1024
        ),
        name="moments",
    )(
        patch_ids, token_counts, alpha_index, patches, pos_table, norm_gain, norm_bias,
        branch_scale, act_range, weight_range,
    )
    cov = cov.reshape(nx, BLOCK, wide).transpose(1, 0, 2).reshape(1, BLOCK, width)
    return cov.astype(F32), mean


def solution(mesh):
    in_specs = (
        P("tok", None),
        P("tok"),
        P(),
        P("tok"),
        P("section", None),
        P("section", None),
        P("section", None),
        P("section", None),
        P("section", None),
        P("section"),
    )
    out_specs = (P("section", None, None), P("section", None))
    return jax.shard_map(body, mesh=mesh, in_specs=in_specs, out_specs=out_specs, check_vma=False)
```

time: 1090 us -> 123 us (0.11)
  the two profiles are of different devices: /device:TPU:1 before, /device:TPU:88 now
where the time goes in v1:
time: 123 us; the launch traced here: 122 us
  Pallas kernels  106 us (86%)
  local copies, waits for them, and re-layouts  13.6 us (11%)
  between operations  1.96 us (2%)
    pallas_call x1, Pallas kernels, body(): pl.pallas_call(functools.partial(kernel, sections, toks), out_shape=(jax....  106 us
    unnamed x17, local copies, waits for them, and re-layouts  8.24 us
    convert_element_type x2, local copies, waits for them, and re-layouts, body(): return (cov.astype(F32), mean)  5.36 us

profile of v1, /device:TPU:88, one launch (start us, length us, event | category | flops | bytes accessed | tf_op | source)
XLA Modules:
  0.0 122.1 jit_solution(6498228708123928225)
XLA Ops:
  1.9 0.0 copy-start
  1.9 1.9 %copy-done = bf16[256,6144]{1,0:T(8,128)(2,1)S(1)} copy-done((bf16[256,6144]{1,0:T(8,128)(2,1)S(1)}, bf16[256,6144]{1,0:T(8,128)(2,1)}, u32[]{:S(2)}) %copy-start) | copy-done | bytes 3145752
  3.8 0.0 copy-start.1
  3.8 1.4 %copy-done.1 = bf16[128,6144]{1,0:T(8,128)(2,1)S(1)} copy-done((bf16[128,6144]{1,0:T(8,128)(2,1)S(1)}, bf16[128,6144]{1,0:T(8,128)(2,1)}, u32[]{:S(2)}) %copy-start.1) | copy-done | bytes 1572888
  5.2 0.0 copy-start.2
  5.2 0.7 copy-done.2
  6.0 0.0 copy-start.3
  6.0 0.7 copy-done.3
  6.7 0.0 copy-start.4
  6.7 0.7 copy-done.4
  7.4 0.0 copy-start.5
  7.4 0.7 copy-done.5
  8.2 0.0 copy-start.6
  8.2 0.7 copy-done.6
  8.9 0.0 copy-start.7
  8.9 0.7 copy-done.7
  9.6 106.1 %moments.1 = (bf16[4,8,16,1536]{3,2,1,0:T(8,128)(2,1)S(1)}, f32[1,6144]{1,0:T(1,128)S(1)}) custom-call(s32[128]{0:T(128)S(1)} %copy-done.7, s32[1]{0:T(128)S(6)} %copy.14.count, s32[1]{0:T(128)S(6)} %copy.15.alpha, bf16[128,6144]{1,0:T(8,128)(2,1)S(1)} %copy-done.1, bf16[256,6144]{1,0:T(8,128)(2,1)S(1)} %copy-done, f32[1,6144]{1,0:T(1,128)S(1)} %copy-done.2, ...), custom_call_target="tpu_custom_call" | custom-call | tf_op jit(solution)/shard_map/moments/pallas_call | solution.py:443
  115.6 0.5 convert_bitcast_fusion
  116.1 2.0 %copy.12 = f32[128,4,1536]{2,1,0:T(4,128)S(1)} copy(f32[128,4,1536]{2,0,1:T(8,128)S(1)} %convert_bitcast_fusion) | data formatting | bytes 6291456 | tf_op jit(solution)/shard_map/convert_element_type | solution.py:501
  118.2 3.3 %reshape.22 = f32[1,128,6144]{2,1,0:T(8,128)} reshape(f32[128,4,1536]{2,1,0:T(4,128)S(1)} %copy.12) | data formatting | bytes 6291456 | tf_op jit(solution)/shard_map/convert_element_type | solution.py:501
  121.5 0.6 copy.16
Async XLA Ops:
  1.9 1.9 %copy-start = (bf16[256,6144]{1,0:T(8,128)(2,1)S(1)}, bf16[256,6144]{1,0:T(8,128)(2,1)}, u32[]{:S(2)}) copy-start(bf16[256,6144]{1,0:T(8,128)(2,1)} %table.1) | copy-start | bytes 9437188
  3.8 1.4 %copy-start.1 = (bf16[128,6144]{1,0:T(8,128)(2,1)S(1)}, bf16[128,6144]{1,0:T(8,128)(2,1)}, u32[]{:S(2)}) copy-start(bf16[128,6144]{1,0:T(8,128)(2,1)} %patches.1) | copy-start | bytes 4718596
  5.2 0.7 copy-start.2
  6.0 0.7 copy-start.3
  6.7 0.7 copy-start.4
  7.4 0.7 copy-start.5
  8.2 0.7 copy-start.6
  8.9 0.7 copy-start.7

commit v2 on v0

v2 whole, which is shorter than its diff:
```python
import functools

import jax
import jax.numpy as jnp
from jax import lax
from jax.experimental import pallas as pl
from jax.experimental.pallas import tpu as pltpu
from jax.sharding import PartitionSpec as P

BLOCK = 128
RING_X = 4
STEP = 512
CHUNKS = 4
EARLY = 1
F32 = jnp.float32
BF16 = jnp.bfloat16
MESH = pl.DeviceIdType.MESH
CONTRACT_ROWS = (((0,), (0,)), ((), ()))


def columns(c, size=STEP):
    return pl.ds(pl.multiple_of(c * size, size), size)


def fold_lanes(values):
    total = values[:, :128]
    for k in range(1, values.shape[1] // 128):
        total = total + values[:, k * 128:(k + 1) * 128]
    return total


def others(size, me, fn):
    def go(k, _):
        fn(lax.rem(me + k, size))
        return 0

    lax.fori_loop(1, size, go, 0)


def merge_means(means, size, wide, spread):
    rows_of = [means[k] for k in range(size)]
    counts = [one[:, wide + BLOCK:wide + BLOCK + 1] for one in rows_of]
    joined = functools.reduce(jnp.add, counts)
    middle = functools.reduce(
        jnp.add, [one[:, :wide + BLOCK] * n for one, n in zip(rows_of, counts)]
    ) / joined
    index = lax.broadcasted_iota(jnp.int32, (8, wide + BLOCK), 0)
    away = jnp.zeros((8, wide + BLOCK), F32)
    weight_of = jnp.zeros((8, 1), F32)
    index_one = lax.broadcasted_iota(jnp.int32, (8, 1), 0)
    for k in range(size):
        away = jnp.where(index == k, rows_of[k][:, :wide + BLOCK] - middle, away)
        weight_of = jnp.where(index_one == k, counts[k], weight_of)
    pushed = away[:, wide:] * weight_of
    spread[...] = lax.dot_general(
        pushed, away[:, :wide], CONTRACT_ROWS,
        precision=lax.Precision.HIGHEST, preferred_element_type=F32,
    )
    return joined, middle


def kernel(
    sections, toks, ids, count, alpha, patches, table, gain, bias, scale, act, weight, out_cov,
    out_mean, own_patches, table_here, ranges, params, hidden, smooth, tokens, gram, mean_send,
    gram_x, mean_x, part_z, mean_z_send, gram_z, mean_z, spread, slab, full, mean_part, mean_full,
    load_sem, par_send, par_pass, par_recv, smo_send, smo_recv, rsx_send, rsx_recv, rmx_send,
    rmx_recv, rsz_send, rsz_recv, rmz_send, rmz_recv, agz_send, agz_recv, agx_send, agx_recv,
    agm_send, agm_recv, store_sem, mean_sem,
):
    s = lax.axis_index("section")
    t = lax.axis_index("tok")
    ny = sections // 2
    nx = RING_X
    nz = toks // nx
    y = lax.div(s, 2)
    core = lax.rem(s, 2)
    partner = s + 1 - 2 * core
    x = lax.rem(t, nx)
    z = lax.div(t, nx)
    width = patches.shape[1]
    rows = patches.shape[0] // sections
    part = width // CHUNKS
    wide = part // nx
    slim = BLOCK // nz
    steps = width // STEP

    def to_section(other):
        return {"section": other, "tok": t}

    def to_x(other):
        return {"section": s, "tok": z * nx + other}

    def to_z(other):
        return {"section": s, "tok": other * nx + x}

    def remote(src, dst, send, recv, where):
        return pltpu.make_async_remote_copy(
            src_ref=src, dst_ref=dst, send_sem=send, recv_sem=recv, device_id=where,
            device_id_type=MESH,
        )

    loads = [
        pltpu.make_async_copy(act, ranges.at[0], load_sem.at[0]),
        pltpu.make_async_copy(weight, ranges.at[1], load_sem.at[1]),
        pltpu.make_async_copy(gain, params.at[s, 0], load_sem.at[2]),
        pltpu.make_async_copy(bias, params.at[s, 1], load_sem.at[3]),
        pltpu.make_async_copy(scale, params.at[s, 2], load_sem.at[4]),
        pltpu.make_async_copy(
            patches.at[pl.ds(pl.multiple_of(s * rows, rows), rows)], own_patches, load_sem.at[5]
        ),
        pltpu.make_async_copy(table, table_here, load_sem.at[6]),
    ]
    for load in loads:
        load.start()

    barrier = pltpu.get_barrier_semaphore()

    def greet(where):
        pl.semaphore_signal(barrier, inc=1, device_id=where, device_id_type=MESH)

    others(sections, s, lambda k: greet(to_section(k)))
    others(nx, x, lambda k: greet(to_x(k)))
    others(nz, z, lambda k: greet(to_z(k)))

    loads[0].wait()
    loads[1].wait()
    exponent = jnp.full((1, STEP), alpha[0], jnp.int32).astype(F32) / 8.0

    def factor_step(c, _):
        cols = columns(c)
        log_factor = exponent * jnp.log(ranges[0, :, cols]) + (exponent - 1.0) * jnp.log(
            ranges[1, :, cols]
        )
        params[s, 3, :, cols] = jnp.exp(-log_factor)
        return 0

    lax.fori_loop(0, steps, factor_step, 0)
    for load in loads[2:5]:
        load.wait()
    pl.semaphore_wait(barrier, sections - 1 + nx - 1 + nz - 1)

    def params_copy(layer, other, send):
        return remote(
            params.at[layer], params.at[layer], send, par_recv.at[layer], to_section(other)
        )

    def params_across(k):
        return params_copy(s, 2 * k + core, par_send.at[k])

    def params_over():
        return params_copy(s, partner, par_send.at[y])

    def params_on(layer):
        return params_copy(layer, partner, par_pass.at[lax.div(layer, 2)])

    others(ny, y, lambda k: params_across(k).start())
    params_over().start()

    def pass_on(layer):
        @pl.when(jnp.logical_and(layer < sections, layer != s))
        def _():
            params_on(layer).wait_recv()
            params_on(layer).start()

    loads[5].wait()
    loads[6].wait()
    patch = lax.broadcasted_iota(jnp.int32, (rows, table.shape[0]), 1)
    row = lax.broadcasted_iota(jnp.int32, (rows, table.shape[0]), 0)
    wanted = jnp.zeros((rows, table.shape[0]), jnp.int32)
    for r in range(rows):
        wanted = jnp.where(row == r, ids[s * rows + r], wanted)
    pick = (patch == wanted).astype(F32).astype(BF16)

    def start_step(c, total):
        cols = columns(c)
        looked_up = jnp.dot(pick, table_here[:, cols], preferred_element_type=F32)
        first = (own_patches[:, cols].astype(F32) + looked_up).astype(BF16).astype(F32)
        hidden[:, cols] = first
        return total + fold_lanes(first)

    no_total = jnp.zeros((rows, 128), F32)
    first_total = lax.fori_loop(0, steps, start_step, no_total)
    pass_on(core)

    def smooth_copy(c, layer, source):
        return remote(
            smooth.at[c, layer], tokens.at[c, source], smo_send.at[c, layer],
            smo_recv.at[c, source], to_section(layer),
        )

    def layer_step(layer, total):
        mine = lax.rem(layer, 2) == core

        @pl.when(mine)
        def _():
            pass_on(layer + 2)

        @pl.when(jnp.logical_not(mine))
        def _():
            params_on(layer).wait_recv()

        centre = jnp.sum(total, axis=1, keepdims=True) * (1.0 / width)

        def spread_step(c, squares):
            away = hidden[:, columns(c)] - centre
            return squares + fold_lanes(away * away)

        squares = lax.fori_loop(0, steps, spread_step, no_total)
        variance = jnp.sum(squares, axis=1, keepdims=True) * (1.0 / width)
        inverse = lax.rsqrt(variance + 1e-06)
        new_total = no_total
        for c in range(CHUNKS):

            def value_step(k, so_far, c=c):
                cols = pl.ds(pl.multiple_of(c * part + k * STEP, STEP), STEP)
                current = hidden[:, cols]
                normed = (current - centre) * inverse * params[layer, 0, :, cols] + params[
                    layer, 1, :, cols
                ]
                smooth[c, layer, :, columns(k)] = (normed * params[layer, 3, :, cols]).astype(BF16)
                inner = normed * (
                    0.7978845608028654 + 0.035677408136300125 * (normed * normed)
                )
                branch = 0.5 * normed * (1.0 + jnp.tanh(inner))
                updated = (current + params[layer, 2, :, cols] * branch).astype(BF16).astype(F32)
                hidden[:, cols] = updated
                return so_far + fold_lanes(updated)

            new_total = lax.fori_loop(0, part // STEP, value_step, new_total)
            if c < EARLY:

                @pl.when(layer != s)
                def _(c=c):
                    smooth_copy(c, layer, s).start()

        return new_total

    lax.fori_loop(0, sections, layer_step, first_total)
    for c in range(CHUNKS):
        if c >= EARLY:
            others(sections, s, lambda k: smooth_copy(c, k, s).start())
        tokens[c, s] = smooth[c, s]

    shard_rows = sections * rows
    used = jnp.full((1, 128), count[0], jnp.int32).astype(F32)
    share = 1.0 / used[:, :1]
    position = lax.broadcasted_iota(jnp.int32, (shard_rows, 128), 0)
    valid = (position < count[0]).astype(F32).astype(BF16)
    across = lax.broadcasted_iota(jnp.int32, (16, shard_rows), 1)
    valid_row = (across < count[0]).astype(F32).astype(BF16)
    kept = {}

    def rsx(c, target, source):
        where = to_x(target)
        return (
            remote(gram.at[c, target], gram_x.at[c, source], rsx_send.at[c, target],
                   rsx_recv.at[c, source], where),
            remote(mean_send.at[c, target], mean_x.at[c, source], rmx_send.at[c, target],
                   rmx_recv.at[c, source], where),
        )

    def rsz(c, target, source):
        where = to_z(target)
        return (
            remote(part_z.at[c, target], gram_z.at[c, source], rsz_send.at[c, target],
                   rsz_recv.at[c, source], where),
            remote(mean_z_send.at[c], mean_z.at[c, source], rmz_send.at[c, target],
                   rmz_recv.at[c, source], where),
        )

    def agz(c, target, source):
        rows_of = slab.at[c, pl.ds(pl.multiple_of(source * slim, slim), slim)]
        return remote(rows_of, rows_of, agz_send.at[c, target], agz_recv.at[c, source],
                      to_z(target))

    def agx(c, target, source):
        return remote(slab.at[c], full.at[c, source], agx_send.at[c, target],
                      agx_recv.at[c, source], to_x(target))

    def agm(target, source):
        return remote(mean_part.at[source], mean_part.at[source], agm_send.at[target],
                      agm_recv.at[source], to_x(target))

    def store(c, source, held):
        cols = pl.ds(pl.multiple_of(c * part + source * wide, wide), wide)
        return pltpu.make_async_copy(held, out_cov.at[:, cols], store_sem.at[c, source])

    def start_both(pair):
        pair[0].start()
        pair[1].start()

    def recv_both(pair):
        pair[0].wait_recv()
        pair[1].wait_recv()

    def gram_stage(c):
        others(sections, s, lambda k: smooth_copy(c, s, k).wait_recv())
        if c == 0:
            block = tokens[c, :, :, :BLOCK].reshape(shard_rows, BLOCK) * valid
            block_sum = lax.dot_general(block, valid, CONTRACT_ROWS, preferred_element_type=F32)
            kept["block"] = block
            kept["sum"] = block_sum[:, :1]
        for k in range(nx):
            here = tokens[c, :, :, k * wide:(k + 1) * wide].reshape(shard_rows, wide)
            mean_here = jnp.dot(valid_row, here, preferred_element_type=F32)[:1] * share
            if c == 0 and k == 0:
                kept["mean"] = mean_here[:, :BLOCK]
            moments = lax.dot_general(
                kept["block"], here, CONTRACT_ROWS, preferred_element_type=F32
            )
            gram[c, k] = (moments - kept["sum"] * mean_here).astype(BF16)
            mean_send[c, k, :, :wide] = mean_here
            mean_send[c, k, :, wide:wide + BLOCK] = kept["mean"]
            mean_send[c, k, :, wide + BLOCK:] = used
        others(nx, x, lambda k: start_both(rsx(c, k, x)))
        mean_x[c, x] = mean_send[c, x]

    def x_stage(c):
        others(nx, x, lambda k: recv_both(rsx(c, x, k)))
        joined, middle = merge_means(mean_x.at[c], nx, wide, spread.at[0])
        mean_z_send[c, :, :wide + BLOCK] = middle
        mean_z_send[c, :, wide + BLOCK:] = jnp.broadcast_to(joined, (1, BLOCK))

        def join(k, _):
            here = pl.ds(pl.multiple_of(k * slim, slim), slim)
            total = spread[0, here, :] + gram[c, x, here, :].astype(F32)
            for j in range(1, nx):
                total = total + gram_x[c, lax.rem(x + j, nx), here, :].astype(F32)
            part_z[c, k] = total.astype(BF16)
            return 0

        lax.fori_loop(0, nz, join, 0)
        others(nz, z, lambda k: start_both(rsz(c, k, z)))
        mean_z[c, z] = mean_z_send[c]
        gram_z[c, z] = part_z[c, z]

    def z_stage(c):
        others(nz, z, lambda k: recv_both(rsz(c, z, k)))
        joined, middle = merge_means(mean_z.at[c], nz, wide, spread.at[1])
        here = pl.ds(pl.multiple_of(z * slim, slim), slim)
        total = spread[1, here, :]
        for k in range(nz):
            total = total + gram_z[c, k].astype(F32)
        slab[c, here, :] = (total / joined).astype(BF16)
        mean_part[x, :, c * wide:(c + 1) * wide] = middle[:, :wide]
        others(nz, z, lambda k: agz(c, k, z).start())
        if c == CHUNKS - 1:
            others(nx, x, lambda k: agm(k, x).start())

    def a_stage(c):
        others(nz, z, lambda k: agz(c, z, k).wait_recv())
        others(nx, x, lambda k: agx(c, k, x).start())
        store(c, x, slab.at[c]).start()

    def b_stage(c):
        def arrived(k):
            agx(c, x, k).wait_recv()
            store(c, k, full.at[c, k]).start()

        others(nx, x, arrived)

    stages = (gram_stage, x_stage, z_stage, a_stage, b_stage)
    for tick in range(CHUNKS + len(stages) - 1):
        for place, stage in enumerate(stages):
            if 0 <= tick - place < CHUNKS:
                stage(tick - place)

    others(nx, x, lambda k: agm(x, k).wait_recv())
    for k in range(nx):
        for c in range(CHUNKS):
            place = c * part + k * wide
            mean_full[:, place:place + wide] = mean_part[k, :, c * wide:(c + 1) * wide]
    mean_store = pltpu.make_async_copy(mean_full, out_mean, mean_sem.at[0])
    mean_store.start()

    others(ny, y, lambda k: params_across(k).wait_send())
    params_over().wait_send()
    others(ny, y, lambda k: params_on(2 * k + core).wait_send())
    others(nx, x, lambda k: agm(k, x).wait_send())

    def finish(c, _):
        def end_x(k):
            rsx(c, k, x)[0].wait_send()
            rsx(c, k, x)[1].wait_send()
            agx(c, k, x).wait_send()
            store(c, k, full.at[c, k]).wait()

        def end_z(k):
            rsz(c, k, z)[0].wait_send()
            rsz(c, k, z)[1].wait_send()
            agz(c, k, z).wait_send()

        others(sections, s, lambda k: smooth_copy(c, k, s).wait_send())
        others(nx, x, end_x)
        others(nz, z, end_z)
        store(c, x, slab.at[c]).wait()
        return 0

    lax.fori_loop(0, CHUNKS, finish, 0)
    mean_store.wait()


def body(
    patches, patch_ids, pos_table, token_counts, norm_gain, norm_bias, branch_scale, act_range,
    weight_range, alpha_index,
):
    sections = lax.axis_size("section")
    toks = lax.axis_size("tok")
    nx, nz = RING_X, toks // RING_X
    width = patches.shape[1]
    rows = patches.shape[0] // sections
    part = width // CHUNKS
    wide = part // nx
    slim = BLOCK // nz
    meta = wide + 2 * BLOCK
    dma = pltpu.SemaphoreType.DMA
    smem = pl.BlockSpec(memory_space=pltpu.SMEM)
    hbm = pl.BlockSpec(memory_space=pl.ANY)
    vmem = pltpu.VMEM
    by_x, by_z = dma((CHUNKS, nx)), dma((CHUNKS, nz))
    by_section = dma((CHUNKS, sections))
    cov, mean = pl.pallas_call(
        functools.partial(kernel, sections, toks),
        out_shape=(
            jax.ShapeDtypeStruct((BLOCK, width), BF16),
            jax.ShapeDtypeStruct((1, width), F32),
        ),
        in_specs=[smem] * 3 + [hbm] * 7,
        out_specs=(hbm, hbm),
        scratch_shapes=[
            vmem((rows, width), BF16),
            vmem(pos_table.shape, BF16),
            vmem((2, 1, width), F32),
            vmem((sections, 4, 1, width), F32),
            vmem((rows, width), F32),
            vmem((CHUNKS, sections, rows, part), BF16),
            vmem((CHUNKS, sections, rows, part), BF16),
            vmem((CHUNKS, nx, BLOCK, wide), BF16),
            vmem((CHUNKS, nx, 1, meta), F32),
            vmem((CHUNKS, nx, BLOCK, wide), BF16),
            vmem((CHUNKS, nx, 1, meta), F32),
            vmem((CHUNKS, nz, slim, wide), BF16),
            vmem((CHUNKS, 1, meta), F32),
            vmem((CHUNKS, nz, slim, wide), BF16),
            vmem((CHUNKS, nz, 1, meta), F32),
            vmem((2, BLOCK, wide), F32),
            vmem((CHUNKS, BLOCK, wide), BF16),
            vmem((CHUNKS, nx, BLOCK, wide), BF16),
            vmem((nx, 1, CHUNKS * wide), F32),
            vmem((1, width), F32),
            dma((7,)),
            dma((sections // 2,)),
            dma((sections // 2,)),
            dma((sections,)),
            by_section,
            by_section,
            by_x, by_x, by_x, by_x,
            by_z, by_z, by_z, by_z,
            by_z, by_z,
            by_x, by_x,
            dma((nx,)),
            dma((nx,)),
            by_x,
            dma((1,)),
        ],
        compiler_params=pltpu.CompilerParams(
            collective_id=0, has_side_effects=True, vmem_limit_bytes=60 * 1024 * 1024
        ),
        name="moments",
    )(
        patch_ids, token_counts, alpha_index, patches, pos_table, norm_gain, norm_bias,
        branch_scale, act_range, weight_range,
    )
    return cov[None].astype(F32), mean


def solution(mesh):
    in_specs = (
        P("tok", None),
        P("tok"),
        P(),
        P("tok"),
        P("section", None),
        P("section", None),
        P("section", None),
        P("section", None),
        P("section", None),
        P("section"),
    )
    out_specs = (P("section", None, None), P("section", None))
    return jax.shard_map(body, mesh=mesh, in_specs=in_specs, out_specs=out_specs, check_vma=False)
```

time: 1090 us -> 78.6 us (0.07)
  waiting for transfers between devices: 540 us -> 0 us
  other arithmetic: 233 us -> 3.4 us
  blocking collectives: 105 us -> 0 us
  local copies, waits for them, and re-layouts: 81.1 us -> 0.61 us
  Pallas kernels: 0 us -> 71.9 us
  loops' own time: 60.9 us -> 0 us
  starting transfers between devices: 48.4 us -> 0 us
  between operations: 15.5 us -> 1.94 us
    all_gather x1 -> x0, waiting for transfers between devices: 527 us -> none  [combined_all(): everything = jax.tree.map(lambda part: lax.all_gather(part, axis), shard)]
    add x62 -> x0, other arithmetic: 159 us -> none  [the longest x31 159 us: combine_moments(): first_gram + second_gram]
    pallas_call x0 -> x1, Pallas kernels: none -> 71.9 us  [body(): pl.pallas_call(functools.partial(kernel, sections, toks), out_shape=(jax....]
    dynamic_slice x73 -> x0, local copies, waits for them, and re-layouts: 68.7 us -> none  [the longest x62 49.2 us: hop(): return combine(so_far, jax.tree.map(lambda part: part[k], everything))]
    another operation x2 -> x0, loops' own time: 60.9 us -> none  [the longest x1 60.6 us: combined_all(): return lax.fori_loop(1, lax.axis_size(axis), hop, leading)]
    unnamed x1 -> x0, blocking collectives: 60.1 us -> none
    ppermute x11 -> x0, starting transfers between devices: 48.4 us -> none  [from_behind(): return lax.ppermute(block, axis, route)]
    all_gather x1 -> x0, blocking collectives: 44.8 us -> none  [combined_all(): everything = jax.tree.map(lambda part: lax.all_gather(part, axis), shard)]
  transfers between devices with their start and end apart: 12 -> 0, of which waited for: 12 -> 0; matrix products, arithmetic and copies ran while one was open for 4% -> 0% of each run, Pallas kernels for 0% -> 0%
where the time goes in v2:
time: 78.6 us; the launch traced here: 77.9 us
  Pallas kernels  71.9 us (91%)
  other arithmetic  3.4 us (4%)
  between operations  1.94 us (2%)
    pallas_call x1, Pallas kernels, body(): pl.pallas_call(functools.partial(kernel, sections, toks), out_shape=(jax....  71.9 us
    convert_element_type x1, other arithmetic, body(): return (cov[None].astype(F32), mean)  3.4 us

profile of v2, /device:TPU:1, one launch (start us, length us, event | category | flops | bytes accessed | tf_op | source)
XLA Modules:
  0.0 77.9 jit_solution(11406497465896813051)
XLA Ops:
  1.9 71.9 %moments.1 = (bf16[128,6144]{1,0:T(8,128)(2,1)}, f32[1,6144]{1,0:T(1,128)}) custom-call(s32[128]{0:T(128)} %ids.1, s32[1]{0:T(128)S(6)} %copy.13.count, s32[1]{0:T(128)S(6)} %copy.14.alpha, bf16[128,6144]{1,0:T(8,128)(2,1)} %patches.1, bf16[256,6144]{1,0:T(8,128)(2,1)} %table.1, f32[1,6144]{1,0:T(1,128)} %gain.1, f32[1,6144]{1,0:T(1,128)} %bias.1, ...), custom_call_target="tpu_custom_call" | custom-call | tf_op jit(solution)/shard_map/moments/pallas_call | solution.py:422
  73.8 0.0 copy-start
  73.8 3.4 %bitcast_convert_fusion = f32[1,128,6144]{2,1,0:T(8,128)} fusion(bf16[128,6144]{1,0:T(8,128)(2,1)} %get-tuple-element.4), kind=kLoop, calls=%fused_computation | loop fusion | flops 786432 | bytes 4718592 | tf_op jit(solution)/shard_map/convert_element_type | solution.py:474
  77.2 0.0 copy-done
  77.2 0.6 copy.15
Async XLA Ops:
  73.8 3.4 %copy-start = (f32[1,6144]{1,0:T(1,128)S(1)}, f32[1,6144]{1,0:T(1,128)}, u32[]{:S(2)}) copy-start(f32[1,6144]{1,0:T(1,128)} %get-tuple-element.9) | copy-start | bytes 73732

commit v3 on v2

--- a/solution.py
+++ b/solution.py
@@ -9,9 +9,9 @@
 
 BLOCK = 128
 RING_X = 4
-STEP = 512
+STEP = 768
 CHUNKS = 4
-EARLY = 1
+EARLY = 0
 F32 = jnp.float32
 BF16 = jnp.bfloat16
 MESH = pl.DeviceIdType.MESH
@@ -61,10 +61,10 @@
 
 def kernel(
     sections, toks, ids, count, alpha, patches, table, gain, bias, scale, act, weight, out_cov,
-    out_mean, own_patches, table_here, ranges, params, hidden, smooth, tokens, gram, mean_send,
-    gram_x, mean_x, part_z, mean_z_send, gram_z, mean_z, spread, slab, full, mean_part, mean_full,
-    load_sem, par_send, par_pass, par_recv, smo_send, smo_recv, rsx_send, rsx_recv, rmx_send,
-    rmx_recv, rsz_send, rsz_recv, rmz_send, rmz_recv, agz_send, agz_recv, agx_send, agx_recv,
+    out_mean, own_patches, table_here, ranges, params, hidden, smooth, tokens, counts, valid_row,
+    block, block_sum, block_mean, part_z, mean_z_send, gram_z, mean_z, spread, slab, full,
+    mean_part, mean_full, load_sem, par_send, par_pass, par_recv, cnt_send, cnt_recv, tok_send,
+    tok_recv, rsz_send, rsz_recv, rmz_send, rmz_recv, agz_send, agz_recv, agx_send, agx_recv,
     agm_send, agm_recv, store_sem, mean_sem,
 ):
     s = lax.axis_index("section")
@@ -93,6 +93,9 @@
     def to_z(other):
         return {"section": s, "tok": other * nx + x}
 
+    def drain(held, sem):
+        pltpu.make_async_copy(held, held, sem).wait()
+
     def remote(src, dst, send, recv, where):
         return pltpu.make_async_remote_copy(
             src_ref=src, dst_ref=dst, send_sem=send, recv_sem=recv, device_id=where,
@@ -118,8 +121,12 @@
     def greet(where):
         pl.semaphore_signal(barrier, inc=1, device_id=where, device_id_type=MESH)
 
-    others(sections, s, lambda k: greet(to_section(k)))
-    others(nx, x, lambda k: greet(to_x(k)))
+    def greet_plane(k, _):
+        to = lax.rem(x + lax.rem(k, nx), nx)
+        greet({"section": lax.rem(s + lax.div(k, nx), sections), "tok": z * nx + to})
+        return 0
+
+    lax.fori_loop(1, sections * nx, greet_plane, 0)
     others(nz, z, lambda k: greet(to_z(k)))
 
     loads[0].wait()
@@ -137,7 +144,7 @@
     lax.fori_loop(0, steps, factor_step, 0)
     for load in loads[2:5]:
         load.wait()
-    pl.semaphore_wait(barrier, sections - 1 + nx - 1 + nz - 1)
+    pl.semaphore_wait(barrier, sections * nx - 1 + nz - 1)
 
     def params_copy(layer, other, send):
         return remote(
@@ -155,6 +162,15 @@
 
     others(ny, y, lambda k: params_across(k).start())
     params_over().start()
+    counts[x] = jnp.full((1, 128), count[0], jnp.int32)
+
+    def counts_copy(target, source):
+        return remote(
+            counts.at[source], counts.at[source], cnt_send.at[0], cnt_recv.at[0],
+            to_x(target),
+        )
+
+    others(nx, x, lambda k: counts_copy(k, x).start())
 
     def pass_on(layer):
         @pl.when(jnp.logical_and(layer < sections, layer != s))
@@ -182,11 +198,37 @@
     first_total = lax.fori_loop(0, steps, start_step, no_total)
     pass_on(core)
 
-    def smooth_copy(c, layer, source):
+    def part_cols(c):
+        if c == 0:
+            return pl.ds(0, BLOCK + wide)
+        return pl.ds(BLOCK + c * wide, wide)
+
+    def tok_copy(c, layer, to, source, at):
+        cols = part_cols(c)
         return remote(
-            smooth.at[c, layer], tokens.at[c, source], smo_send.at[c, layer],
-            smo_recv.at[c, source], to_section(layer),
+            smooth.at[layer * nx + to, :, cols], tokens.at[at * sections + source, :, cols],
+            tok_send.at[c], tok_recv.at[c],
+            {"section": layer, "tok": z * nx + to},
         )
+
+    def send_layer(c, layer):
+        def go(k, _):
+            to = lax.rem(x + k, nx)
+
+            @pl.when(jnp.logical_or(layer != s, to != x))
+            def _():
+                tok_copy(c, layer, to, s, x).start()
+
+            return 0
+
+        lax.fori_loop(0, nx, go, 0)
+
+    def all_tok(fn):
+        def go(k, _):
+            fn(lax.rem(s + lax.div(k, nx), sections), lax.rem(x + lax.rem(k, nx), nx))
+            return 0
+
+        lax.fori_loop(1, sections * nx, go, 0)
 
     def layer_step(layer, total):
         mine = lax.rem(layer, 2) == core
@@ -217,7 +259,11 @@
                 normed = (current - centre) * inverse * params[layer, 0, :, cols] + params[
                     layer, 1, :, cols
                 ]
-                smooth[c, layer, :, columns(k)] = (normed * params[layer, 3, :, cols]).astype(BF16)
+                smoothed = (normed * params[layer, 3, :, cols]).astype(BF16)
+                for j in range(STEP // wide):
+                    smooth[layer * nx + k * (STEP // wide) + j, :, BLOCK + c * wide:BLOCK + (c + 1) * wide] = (
+                        smoothed[:, j * wide:(j + 1) * wide]
+                    )
                 inner = normed * (
                     0.7978845608028654 + 0.035677408136300125 * (normed * normed)
                 )
@@ -227,118 +273,94 @@
                 return so_far + fold_lanes(updated)
 
             new_total = lax.fori_loop(0, part // STEP, value_step, new_total)
+            if c == 0:
+                for j in range(nx):
+                    smooth[layer * nx + j, :, :BLOCK] = smooth[layer * nx, :, BLOCK:2 * BLOCK]
             if c < EARLY:
-
-                @pl.when(layer != s)
-                def _(c=c):
-                    smooth_copy(c, layer, s).start()
+                send_layer(c, layer)
 
         return new_total
 
     lax.fori_loop(0, sections, layer_step, first_total)
     for c in range(CHUNKS):
         if c >= EARLY:
-            others(sections, s, lambda k: smooth_copy(c, k, s).start())
-        tokens[c, s] = smooth[c, s]
-
-    shard_rows = sections * rows
-    used = jnp.full((1, 128), count[0], jnp.int32).astype(F32)
-    share = 1.0 / used[:, :1]
-    position = lax.broadcasted_iota(jnp.int32, (shard_rows, 128), 0)
-    valid = (position < count[0]).astype(F32).astype(BF16)
-    across = lax.broadcasted_iota(jnp.int32, (16, shard_rows), 1)
-    valid_row = (across < count[0]).astype(F32).astype(BF16)
-    kept = {}
-
-    def rsx(c, target, source):
-        where = to_x(target)
-        return (
-            remote(gram.at[c, target], gram_x.at[c, source], rsx_send.at[c, target],
-                   rsx_recv.at[c, source], where),
-            remote(mean_send.at[c, target], mean_x.at[c, source], rmx_send.at[c, target],
-                   rmx_recv.at[c, source], where),
-        )
+            all_tok(lambda layer, to, c=c: tok_copy(c, layer, to, s, x).start())
+    tokens[x * sections + s] = smooth[s * nx + x]
+    drain(counts.at[:nx - 1], cnt_recv.at[0])
+
+    group = nx * sections * rows
 
     def rsz(c, target, source):
         where = to_z(target)
         return (
-            remote(part_z.at[c, target], gram_z.at[c, source], rsz_send.at[c, target],
-                   rsz_recv.at[c, source], where),
-            remote(mean_z_send.at[c], mean_z.at[c, source], rmz_send.at[c, target],
-                   rmz_recv.at[c, source], where),
+            remote(part_z.at[c, target], gram_z.at[c, source], rsz_send.at[c], rsz_recv.at[c],
+                   where),
+            remote(mean_z_send.at[c], mean_z.at[c, source], rmz_send.at[c], rmz_recv.at[c],
+                   where),
         )
 
     def agz(c, target, source):
         rows_of = slab.at[c, pl.ds(pl.multiple_of(source * slim, slim), slim)]
-        return remote(rows_of, rows_of, agz_send.at[c, target], agz_recv.at[c, source],
+        return remote(rows_of, rows_of, agz_send.at[c], agz_recv.at[c],
                       to_z(target))
 
     def agx(c, target, source):
-        return remote(slab.at[c], full.at[c, source], agx_send.at[c, target],
-                      agx_recv.at[c, source], to_x(target))
+        return remote(slab.at[c], full.at[c, source], agx_send.at[c],
+                      agx_recv.at[c], to_x(target))
 
     def agm(target, source):
-        return remote(mean_part.at[source], mean_part.at[source], agm_send.at[target],
-                      agm_recv.at[source], to_x(target))
+        return remote(mean_part.at[source], mean_part.at[source], agm_send.at[0],
+                      agm_recv.at[0], to_x(target))
 
     def store(c, source, held):
         cols = pl.ds(pl.multiple_of(c * part + source * wide, wide), wide)
-        return pltpu.make_async_copy(held, out_cov.at[:, cols], store_sem.at[c, source])
+        return pltpu.make_async_copy(held, out_cov.at[:, cols], store_sem.at[c])
 
     def start_both(pair):
         pair[0].start()
         pair[1].start()
 
-    def recv_both(pair):
-        pair[0].wait_recv()
-        pair[1].wait_recv()
-
     def gram_stage(c):
-        others(sections, s, lambda k: smooth_copy(c, s, k).wait_recv())
+        drain(tokens.at[:nx * sections - 1, :, part_cols(c)], tok_recv.at[c])
+        used = functools.reduce(jnp.add, [counts[k] for k in range(nx)]).astype(F32)
         if c == 0:
-            block = tokens[c, :, :, :BLOCK].reshape(shard_rows, BLOCK) * valid
-            block_sum = lax.dot_general(block, valid, CONTRACT_ROWS, preferred_element_type=F32)
-            kept["block"] = block
-            kept["sum"] = block_sum[:, :1]
-        for k in range(nx):
-            here = tokens[c, :, :, k * wide:(k + 1) * wide].reshape(shard_rows, wide)
-            mean_here = jnp.dot(valid_row, here, preferred_element_type=F32)[:1] * share
-            if c == 0 and k == 0:
-                kept["mean"] = mean_here[:, :BLOCK]
-            moments = lax.dot_general(
-                kept["block"], here, CONTRACT_ROWS, preferred_element_type=F32
+            place = lax.broadcasted_iota(jnp.int32, (sections * rows, BLOCK), 0)
+            across = lax.broadcasted_iota(jnp.int32, (16, sections * rows), 1)
+            valid = []
+            for k in range(nx):
+                here = counts[k][:, :1]
+                valid.append((place < here).astype(F32).astype(BF16))
+                valid_row[:, k * sections * rows:(k + 1) * sections * rows] = (
+                    (across < here).astype(F32).astype(BF16)
+                )
+            valid = jnp.concatenate(valid, axis=0)
+            block[...] = tokens[:, :, :BLOCK].reshape(group, BLOCK) * valid
+            block_sum[...] = lax.dot_general(
+                block[...], valid, CONTRACT_ROWS, preferred_element_type=F32
             )
-            gram[c, k] = (moments - kept["sum"] * mean_here).astype(BF16)
-            mean_send[c, k, :, :wide] = mean_here
-            mean_send[c, k, :, wide:wide + BLOCK] = kept["mean"]
-            mean_send[c, k, :, wide + BLOCK:] = used
-        others(nx, x, lambda k: start_both(rsx(c, k, x)))
-        mean_x[c, x] = mean_send[c, x]
-
-    def x_stage(c):
-        others(nx, x, lambda k: recv_both(rsx(c, x, k)))
-        joined, middle = merge_means(mean_x.at[c], nx, wide, spread.at[0])
-        mean_z_send[c, :, :wide + BLOCK] = middle
-        mean_z_send[c, :, wide + BLOCK:] = jnp.broadcast_to(joined, (1, BLOCK))
-
-        def join(k, _):
-            here = pl.ds(pl.multiple_of(k * slim, slim), slim)
-            total = spread[0, here, :] + gram[c, x, here, :].astype(F32)
-            for j in range(1, nx):
-                total = total + gram_x[c, lax.rem(x + j, nx), here, :].astype(F32)
-            part_z[c, k] = total.astype(BF16)
-            return 0
-
-        lax.fori_loop(0, nz, join, 0)
+        here = tokens[:, :, BLOCK + c * wide:BLOCK + (c + 1) * wide].reshape(group, wide)
+        mean_here = jnp.dot(valid_row[...], here, preferred_element_type=F32)[:1] / used[:, :1]
+        if c == 0:
+            first = tokens[:, :, :BLOCK].reshape(group, BLOCK)
+            block_mean[...] = (
+                jnp.dot(valid_row[...], first, preferred_element_type=F32)[:1] / used
+            )
+        moments = lax.dot_general(block[...], here, CONTRACT_ROWS, preferred_element_type=F32)
+        moments = moments - block_sum[:, :1] * mean_here
+        part_z[c] = moments.astype(BF16).reshape(nz, slim, wide)
+        mean_z_send[c, :, :wide] = mean_here
+        mean_z_send[c, :, wide:wide + BLOCK] = block_mean[...]
+        mean_z_send[c, :, wide + BLOCK:] = used
         others(nz, z, lambda k: start_both(rsz(c, k, z)))
         mean_z[c, z] = mean_z_send[c]
         gram_z[c, z] = part_z[c, z]
 
     def z_stage(c):
-        others(nz, z, lambda k: recv_both(rsz(c, z, k)))
-        joined, middle = merge_means(mean_z.at[c], nz, wide, spread.at[1])
+        drain(mean_z.at[c, :nz - 1], rmz_recv.at[c])
+        drain(gram_z.at[c, :nz - 1], rsz_recv.at[c])
+        joined, middle = merge_means(mean_z.at[c], nz, wide, spread)
         here = pl.ds(pl.multiple_of(z * slim, slim), slim)
-        total = spread[1, here, :]
+        total = spread[here, :]
         for k in range(nz):
             total = total + gram_z[c, k].astype(F32)
         slab[c, here, :] = (total / joined).astype(BF16)
@@ -348,24 +370,21 @@
             others(nx, x, lambda k: agm(k, x).start())
 
     def a_stage(c):
-        others(nz, z, lambda k: agz(c, z, k).wait_recv())
+        drain(slab.at[c, :BLOCK - slim], agz_recv.at[c])
         others(nx, x, lambda k: agx(c, k, x).start())
         store(c, x, slab.at[c]).start()
 
     def b_stage(c):
-        def arrived(k):
-            agx(c, x, k).wait_recv()
-            store(c, k, full.at[c, k]).start()
-
-        others(nx, x, arrived)
-
-    stages = (gram_stage, x_stage, z_stage, a_stage, b_stage)
+        drain(full.at[c, :nx - 1], agx_recv.at[c])
+        others(nx, x, lambda k: store(c, k, full.at[c, k]).start())
+
+    stages = (gram_stage, z_stage, a_stage, b_stage)
     for tick in range(CHUNKS + len(stages) - 1):
         for place, stage in enumerate(stages):
             if 0 <= tick - place < CHUNKS:
                 stage(tick - place)
 
-    others(nx, x, lambda k: agm(x, k).wait_recv())
+    drain(mean_part.at[:nx - 1], agm_recv.at[0])
     for k in range(nx):
         for c in range(CHUNKS):
             place = c * part + k * wide
@@ -376,27 +395,17 @@
     others(ny, y, lambda k: params_across(k).wait_send())
     params_over().wait_send()
     others(ny, y, lambda k: params_on(2 * k + core).wait_send())
-    others(nx, x, lambda k: agm(k, x).wait_send())
-
-    def finish(c, _):
-        def end_x(k):
-            rsx(c, k, x)[0].wait_send()
-            rsx(c, k, x)[1].wait_send()
-            agx(c, k, x).wait_send()
-            store(c, k, full.at[c, k]).wait()
-
-        def end_z(k):
-            rsz(c, k, z)[0].wait_send()
-            rsz(c, k, z)[1].wait_send()
-            agz(c, k, z).wait_send()
-
-        others(sections, s, lambda k: smooth_copy(c, k, s).wait_send())
-        others(nx, x, end_x)
-        others(nz, z, end_z)
-        store(c, x, slab.at[c]).wait()
-        return 0
-
-    lax.fori_loop(0, CHUNKS, finish, 0)
+    drain(mean_part.at[:nx - 1], agm_send.at[0])
+
+    drain(counts.at[:nx - 1], cnt_send.at[0])
+
+    for c in range(CHUNKS):
+        drain(smooth.at[:nx * sections - 1, :, part_cols(c)], tok_send.at[c])
+        drain(part_z.at[c, :nz - 1], rsz_send.at[c])
+        drain(mean_z.at[c, :nz - 1], rmz_send.at[c])
+        drain(slab.at[c, :BLOCK - slim], agz_send.at[c])
+        drain(full.at[c, :nx - 1], agx_send.at[c])
+        drain(out_cov.at[:, c * part:(c + 1) * part], store_sem.at[c])
     mean_store.wait()
 
 
@@ -417,8 +426,8 @@
     smem = pl.BlockSpec(memory_space=pltpu.SMEM)
     hbm = pl.BlockSpec(memory_space=pl.ANY)
     vmem = pltpu.VMEM
-    by_x, by_z = dma((CHUNKS, nx)), dma((CHUNKS, nz))
-    by_section = dma((CHUNKS, sections))
+    each = dma((CHUNKS,))
+    group = nx * sections * rows
     cov, mean = pl.pallas_call(
         functools.partial(kernel, sections, toks),
         out_shape=(
@@ -433,17 +442,18 @@
             vmem((2, 1, width), F32),
             vmem((sections, 4, 1, width), F32),
             vmem((rows, width), F32),
-            vmem((CHUNKS, sections, rows, part), BF16),
-            vmem((CHUNKS, sections, rows, part), BF16),
-            vmem((CHUNKS, nx, BLOCK, wide), BF16),
-            vmem((CHUNKS, nx, 1, meta), F32),
-            vmem((CHUNKS, nx, BLOCK, wide), BF16),
-            vmem((CHUNKS, nx, 1, meta), F32),
+            vmem((sections * nx, rows, BLOCK + CHUNKS * wide), BF16),
+            vmem((nx * sections, rows, BLOCK + CHUNKS * wide), BF16),
+            vmem((nx, 1, 128), jnp.int32),
+            vmem((16, group), BF16),
+            vmem((group, BLOCK), BF16),
+            vmem((BLOCK, BLOCK), F32),
+            vmem((1, BLOCK), F32),
             vmem((CHUNKS, nz, slim, wide), BF16),
             vmem((CHUNKS, 1, meta), F32),
             vmem((CHUNKS, nz, slim, wide), BF16),
             vmem((CHUNKS, nz, 1, meta), F32),
-            vmem((2, BLOCK, wide), F32),
+            vmem((BLOCK, wide), F32),
             vmem((CHUNKS, BLOCK, wide), BF16),
             vmem((CHUNKS, nx, BLOCK, wide), BF16),
             vmem((nx, 1, CHUNKS * wide), F32),
@@ -452,15 +462,15 @@
             dma((sections // 2,)),
             dma((sections // 2,)),
             dma((sections,)),
-            by_section,
-            by_section,
-            by_x, by_x, by_x, by_x,
-            by_z, by_z, by_z, by_z,
-            by_z, by_z,
-            by_x, by_x,
-            dma((nx,)),
-            dma((nx,)),
-            by_x,
+            dma((1,)),
+            dma((1,)),
+            each, each,
+            each, each, each, each,
+            each, each,
+            each, each,
+            dma((1,)),
+            dma((1,)),
+            each,
             dma((1,)),
         ],
         compiler_params=pltpu.CompilerParams(

time: 78.6 us -> 73.3 us (0.933)
  Pallas kernels: 71.9 us -> 67.2 us
    pallas_call x1, Pallas kernels: 71.9 us -> 67.2 us  [body(): pl.pallas_call(functools.partial(kernel, sections, toks), out_shape=(jax....]
where the time goes in v3:
time: 73.3 us; the launch traced here: 73.1 us
  Pallas kernels  67.2 us (92%)
  other arithmetic  3.4 us (5%)
  between operations  1.94 us (3%)
    pallas_call x1, Pallas kernels, body(): pl.pallas_call(functools.partial(kernel, sections, toks), out_shape=(jax....  67.2 us
    convert_element_type x1, other arithmetic, body(): return (cov[None].astype(F32), mean)  3.4 us

profile of v3, /device:TPU:1, one launch (start us, length us, event | category | flops | bytes accessed | tf_op | source)
XLA Modules:
  0.0 73.1 jit_solution(14685781338330292477)
XLA Ops:
  1.9 67.2 %moments.1 = (bf16[128,6144]{1,0:T(8,128)(2,1)}, f32[1,6144]{1,0:T(1,128)}) custom-call(s32[128]{0:T(128)} %ids.1, s32[1]{0:T(128)S(6)} %copy.13.count, s32[1]{0:T(128)S(6)} %copy.14.alpha, bf16[128,6144]{1,0:T(8,128)(2,1)} %patches.1, bf16[256,6144]{1,0:T(8,128)(2,1)} %table.1, f32[1,6144]{1,0:T(1,128)} %gain.1, f32[1,6144]{1,0:T(1,128)} %bias.1, ...), custom_call_target="tpu_custom_call" | custom-call | tf_op jit(solution)/shard_map/moments/pallas_call | solution.py:431
  69.1 0.0 copy-start
  69.1 3.4 %bitcast_convert_fusion = f32[1,128,6144]{2,1,0:T(8,128)} fusion(bf16[128,6144]{1,0:T(8,128)(2,1)} %get-tuple-element.4), kind=kLoop, calls=%fused_computation | loop fusion | flops 786432 | bytes 4718592 | tf_op jit(solution)/shard_map/convert_element_type | solution.py:484
  72.5 0.0 copy-done
  72.5 0.6 copy.15
Async XLA Ops:
  69.1 3.4 %copy-start = (f32[1,6144]{1,0:T(1,128)S(1)}, f32[1,6144]{1,0:T(1,128)}, u32[]{:S(2)}) copy-start(f32[1,6144]{1,0:T(1,128)} %get-tuple-element.9) | copy-start | bytes 73732

commit v4 on v3

--- a/solution.py
+++ b/solution.py
@@ -10,8 +10,11 @@
 BLOCK = 128
 RING_X = 4
 STEP = 768
-CHUNKS = 4
-EARLY = 0
+UNITS = (3, 3, 3, 3)
+SWAPPED = ()
+WIDES = [128 * n for n in UNITS]
+STARTS = [sum(WIDES[:k]) for k in range(len(WIDES))]
+CHUNKS = len(WIDES)
 F32 = jnp.float32
 BF16 = jnp.bfloat16
 MESH = pl.DeviceIdType.MESH
@@ -39,33 +42,38 @@
 
 def merge_means(means, size, wide, spread):
     rows_of = [means[k] for k in range(size)]
-    counts = [one[:, wide + BLOCK:wide + BLOCK + 1] for one in rows_of]
+    counts = [one[:, BLOCK:BLOCK + 1] for one in rows_of]
     joined = functools.reduce(jnp.add, counts)
-    middle = functools.reduce(
-        jnp.add, [one[:, :wide + BLOCK] * n for one, n in zip(rows_of, counts)]
-    ) / joined
-    index = lax.broadcasted_iota(jnp.int32, (8, wide + BLOCK), 0)
-    away = jnp.zeros((8, wide + BLOCK), F32)
+
+    def apart(start, extent):
+        pieces = [one[:, start:start + extent] for one in rows_of]
+        middle = functools.reduce(jnp.add, [one * n for one, n in zip(pieces, counts)]) / joined
+        index = lax.broadcasted_iota(jnp.int32, (8, extent), 0)
+        away = jnp.zeros((8, extent), F32)
+        for k in range(size):
+            away = jnp.where(index == k, pieces[k] - middle, away)
+        return away, middle
+
+    index_one = lax.broadcasted_iota(jnp.int32, (8, 1), 0)
     weight_of = jnp.zeros((8, 1), F32)
-    index_one = lax.broadcasted_iota(jnp.int32, (8, 1), 0)
     for k in range(size):
-        away = jnp.where(index == k, rows_of[k][:, :wide + BLOCK] - middle, away)
         weight_of = jnp.where(index_one == k, counts[k], weight_of)
-    pushed = away[:, wide:] * weight_of
-    spread[...] = lax.dot_general(
-        pushed, away[:, :wide], CONTRACT_ROWS,
+    pushed, _ = apart(0, BLOCK)
+    away, middle = apart(2 * BLOCK, wide)
+    spread[:, :wide] = lax.dot_general(
+        pushed * weight_of, away, CONTRACT_ROWS,
         precision=lax.Precision.HIGHEST, preferred_element_type=F32,
     )
     return joined, middle
 
 
 def kernel(
-    sections, toks, ids, count, alpha, patches, table, gain, bias, scale, act, weight, out_cov,
-    out_mean, own_patches, table_here, ranges, params, hidden, smooth, tokens, counts, valid_row,
-    block, block_sum, block_mean, part_z, mean_z_send, gram_z, mean_z, spread, slab, full,
-    mean_part, mean_full, load_sem, par_send, par_pass, par_recv, cnt_send, cnt_recv, tok_send,
+    sections, toks, ids, count, alpha, patches, table, gain, bias, scale, act, weight, final,
+    mean_full, own_patches, table_here, ranges, params, hidden, smooth, tokens, counts, valid_row,
+    block, block_sum, block_mean, part_z, mean_z_send, gram_z, mean_z, spread, mean_part,
+    load_sem, par_send, par_pass, par_recv, cnt_send, cnt_recv, tok_send,
     tok_recv, rsz_send, rsz_recv, rmz_send, rmz_recv, agz_send, agz_recv, agx_send, agx_recv,
-    agm_send, agm_recv, store_sem, mean_sem,
+    agm_send, agm_recv,
 ):
     s = lax.axis_index("section")
     t = lax.axis_index("tok")
@@ -79,8 +87,6 @@
     z = lax.div(t, nx)
     width = patches.shape[1]
     rows = patches.shape[0] // sections
-    part = width // CHUNKS
-    wide = part // nx
     slim = BLOCK // nz
     steps = width // STEP
 
@@ -200,8 +206,17 @@
 
     def part_cols(c):
         if c == 0:
-            return pl.ds(0, BLOCK + wide)
-        return pl.ds(BLOCK + c * wide, wide)
+            return pl.ds(0, BLOCK + WIDES[0])
+        return pl.ds(BLOCK + STARTS[c], WIDES[c])
+
+    def quarter_cols(c):
+        return pl.ds(STARTS[c], WIDES[c])
+
+    def own_cols(c, of):
+        return pl.ds(pl.multiple_of(nx * STARTS[c] + of * WIDES[c], BLOCK), WIDES[c])
+
+    def all_cols(c):
+        return pl.ds(nx * STARTS[c], nx * WIDES[c])
 
     def tok_copy(c, layer, to, source, at):
         cols = part_cols(c)
@@ -211,21 +226,9 @@
             {"section": layer, "tok": z * nx + to},
         )
 
-    def send_layer(c, layer):
-        def go(k, _):
-            to = lax.rem(x + k, nx)
-
-            @pl.when(jnp.logical_or(layer != s, to != x))
-            def _():
-                tok_copy(c, layer, to, s, x).start()
-
-            return 0
-
-        lax.fori_loop(0, nx, go, 0)
-
     def all_tok(fn):
         def go(k, _):
-            fn(lax.rem(s + lax.div(k, nx), sections), lax.rem(x + lax.rem(k, nx), nx))
+            fn(lax.rem(s + lax.rem(k, sections), sections), lax.rem(x + lax.div(k, sections), nx))
             return 0
 
         lax.fori_loop(1, sections * nx, go, 0)
@@ -252,39 +255,31 @@
         inverse = lax.rsqrt(variance + 1e-06)
         new_total = no_total
         for c in range(CHUNKS):
-
-            def value_step(k, so_far, c=c):
-                cols = pl.ds(pl.multiple_of(c * part + k * STEP, STEP), STEP)
+            for j in range(nx):
+                start = nx * STARTS[c] + j * WIDES[c]
+                cols = slice(start, start + WIDES[c])
                 current = hidden[:, cols]
                 normed = (current - centre) * inverse * params[layer, 0, :, cols] + params[
                     layer, 1, :, cols
                 ]
                 smoothed = (normed * params[layer, 3, :, cols]).astype(BF16)
-                for j in range(STEP // wide):
-                    smooth[layer * nx + k * (STEP // wide) + j, :, BLOCK + c * wide:BLOCK + (c + 1) * wide] = (
-                        smoothed[:, j * wide:(j + 1) * wide]
-                    )
+                place = BLOCK + STARTS[c]
+                smooth[layer * nx + j, :, place:place + WIDES[c]] = smoothed
+                if c == 0 and j == 0:
+                    for k in range(nx):
+                        smooth[layer * nx + k, :, :BLOCK] = smoothed[:, :BLOCK]
                 inner = normed * (
                     0.7978845608028654 + 0.035677408136300125 * (normed * normed)
                 )
                 branch = 0.5 * normed * (1.0 + jnp.tanh(inner))
                 updated = (current + params[layer, 2, :, cols] * branch).astype(BF16).astype(F32)
                 hidden[:, cols] = updated
-                return so_far + fold_lanes(updated)
-
-            new_total = lax.fori_loop(0, part // STEP, value_step, new_total)
-            if c == 0:
-                for j in range(nx):
-                    smooth[layer * nx + j, :, :BLOCK] = smooth[layer * nx, :, BLOCK:2 * BLOCK]
-            if c < EARLY:
-                send_layer(c, layer)
-
+                new_total = new_total + fold_lanes(updated)
         return new_total
 
     lax.fori_loop(0, sections, layer_step, first_total)
     for c in range(CHUNKS):
-        if c >= EARLY:
-            all_tok(lambda layer, to, c=c: tok_copy(c, layer, to, s, x).start())
+        all_tok(lambda layer, to, c=c: tok_copy(c, layer, to, s, x).start())
     tokens[x * sections + s] = smooth[s * nx + x]
     drain(counts.at[:nx - 1], cnt_recv.at[0])
 
@@ -292,29 +287,36 @@
 
     def rsz(c, target, source):
         where = to_z(target)
+        cols = quarter_cols(c)
+        meta = pl.ds(0, 2 * BLOCK + WIDES[c])
         return (
-            remote(part_z.at[c, target], gram_z.at[c, source], rsz_send.at[c], rsz_recv.at[c],
-                   where),
-            remote(mean_z_send.at[c], mean_z.at[c, source], rmz_send.at[c], rmz_recv.at[c],
-                   where),
+            remote(part_z.at[target, :, cols], gram_z.at[source, :, cols], rsz_send.at[c],
+                   rsz_recv.at[c], where),
+            remote(mean_z_send.at[c, :, meta], mean_z.at[c, source, :, meta], rmz_send.at[c],
+                   rmz_recv.at[c], where),
         )
 
-    def agz(c, target, source):
-        rows_of = slab.at[c, pl.ds(pl.multiple_of(source * slim, slim), slim)]
-        return remote(rows_of, rows_of, agz_send.at[c], agz_recv.at[c],
-                      to_z(target))
-
-    def agx(c, target, source):
-        return remote(slab.at[c], full.at[c, source], agx_send.at[c],
-                      agx_recv.at[c], to_x(target))
+    def along_z(c, target):
+        cols = all_cols(c) if c in SWAPPED else own_cols(c, x)
+        held = final.at[z, :, cols]
+        return remote(held, held, agz_send.at[c], agz_recv.at[c], to_z(target))
+
+    def along_x(c, target):
+        cols = own_cols(c, x)
+        held = final.at[z, :, cols] if c in SWAPPED else final.at[:, :, cols]
+        return remote(held, held, agx_send.at[c], agx_recv.at[c], to_x(target))
+
+    def drain_z(c, sem):
+        size = nx * WIDES[c] if c in SWAPPED else WIDES[c]
+        drain(final.at[:nz - 1, :, :size], sem.at[c])
+
+    def drain_x(c, sem):
+        size = (nx - 1) * WIDES[c]
+        drain(final.at[0, :, :size] if c in SWAPPED else final.at[:, :, :size], sem.at[c])
 
     def agm(target, source):
         return remote(mean_part.at[source], mean_part.at[source], agm_send.at[0],
                       agm_recv.at[0], to_x(target))
-
-    def store(c, source, held):
-        cols = pl.ds(pl.multiple_of(c * part + source * wide, wide), wide)
-        return pltpu.make_async_copy(held, out_cov.at[:, cols], store_sem.at[c])
 
     def start_both(pair):
         pair[0].start()
@@ -338,7 +340,8 @@
             block_sum[...] = lax.dot_general(
                 block[...], valid, CONTRACT_ROWS, preferred_element_type=F32
             )
-        here = tokens[:, :, BLOCK + c * wide:BLOCK + (c + 1) * wide].reshape(group, wide)
+        wide, start = WIDES[c], STARTS[c]
+        here = tokens[:, :, BLOCK + start:BLOCK + start + wide].reshape(group, wide)
         mean_here = jnp.dot(valid_row[...], here, preferred_element_type=F32)[:1] / used[:, :1]
         if c == 0:
             first = tokens[:, :, :BLOCK].reshape(group, BLOCK)
@@ -347,36 +350,44 @@
             )
         moments = lax.dot_general(block[...], here, CONTRACT_ROWS, preferred_element_type=F32)
         moments = moments - block_sum[:, :1] * mean_here
-        part_z[c] = moments.astype(BF16).reshape(nz, slim, wide)
-        mean_z_send[c, :, :wide] = mean_here
-        mean_z_send[c, :, wide:wide + BLOCK] = block_mean[...]
-        mean_z_send[c, :, wide + BLOCK:] = used
+        part_z[:, :, start:start + wide] = moments.astype(BF16).reshape(nz, slim, wide)
+        mean_z_send[c, :, :BLOCK] = block_mean[...]
+        mean_z_send[c, :, BLOCK:2 * BLOCK] = used
+        mean_z_send[c, :, 2 * BLOCK:2 * BLOCK + wide] = mean_here
         others(nz, z, lambda k: start_both(rsz(c, k, z)))
         mean_z[c, z] = mean_z_send[c]
-        gram_z[c, z] = part_z[c, z]
+        gram_z[z, :, start:start + wide] = part_z[z, :, start:start + wide]
 
     def z_stage(c):
-        drain(mean_z.at[c, :nz - 1], rmz_recv.at[c])
-        drain(gram_z.at[c, :nz - 1], rsz_recv.at[c])
+        wide, start = WIDES[c], STARTS[c]
+        drain(mean_z.at[c, :nz - 1, :, :2 * BLOCK + wide], rmz_recv.at[c])
+        drain(gram_z.at[:nz - 1, :, :wide], rsz_recv.at[c])
         joined, middle = merge_means(mean_z.at[c], nz, wide, spread)
-        here = pl.ds(pl.multiple_of(z * slim, slim), slim)
-        total = spread[here, :]
+        total = spread[pl.ds(pl.multiple_of(z * slim, slim), slim), :wide]
         for k in range(nz):
-            total = total + gram_z[c, k].astype(F32)
-        slab[c, here, :] = (total / joined).astype(BF16)
-        mean_part[x, :, c * wide:(c + 1) * wide] = middle[:, :wide]
-        others(nz, z, lambda k: agz(c, k, z).start())
+            total = total + gram_z[k, :, start:start + wide].astype(F32)
+        final[z, :, own_cols(c, x)] = (total / joined).astype(BF16)
+        mean_part[x, :, start:start + wide] = middle
+        if c in SWAPPED:
+            others(nx, x, lambda k: along_x(c, k).start())
+        else:
+            others(nz, z, lambda k: along_z(c, k).start())
         if c == CHUNKS - 1:
             others(nx, x, lambda k: agm(k, x).start())
 
     def a_stage(c):
-        drain(slab.at[c, :BLOCK - slim], agz_recv.at[c])
-        others(nx, x, lambda k: agx(c, k, x).start())
-        store(c, x, slab.at[c]).start()
+        if c in SWAPPED:
+            drain_x(c, agx_recv)
+            others(nz, z, lambda k: along_z(c, k).start())
+        else:
+            drain_z(c, agz_recv)
+            others(nx, x, lambda k: along_x(c, k).start())
 
     def b_stage(c):
-        drain(full.at[c, :nx - 1], agx_recv.at[c])
-        others(nx, x, lambda k: store(c, k, full.at[c, k]).start())
+        if c in SWAPPED:
+            drain_z(c, agz_recv)
+        else:
+            drain_x(c, agx_recv)
 
     stages = (gram_stage, z_stage, a_stage, b_stage)
     for tick in range(CHUNKS + len(stages) - 1):
@@ -387,10 +398,9 @@
     drain(mean_part.at[:nx - 1], agm_recv.at[0])
     for k in range(nx):
         for c in range(CHUNKS):
-            place = c * part + k * wide
-            mean_full[:, place:place + wide] = mean_part[k, :, c * wide:(c + 1) * wide]
-    mean_store = pltpu.make_async_copy(mean_full, out_mean, mean_sem.at[0])
-    mean_store.start()
+            start, wide = STARTS[c], WIDES[c]
+            place = nx * start + k * wide
+            mean_full[:, place:place + wide] = mean_part[k, :, start:start + wide]
 
     others(ny, y, lambda k: params_across(k).wait_send())
     params_over().wait_send()
@@ -401,12 +411,10 @@
 
     for c in range(CHUNKS):
         drain(smooth.at[:nx * sections - 1, :, part_cols(c)], tok_send.at[c])
-        drain(part_z.at[c, :nz - 1], rsz_send.at[c])
-        drain(mean_z.at[c, :nz - 1], rmz_send.at[c])
-        drain(slab.at[c, :BLOCK - slim], agz_send.at[c])
-        drain(full.at[c, :nx - 1], agx_send.at[c])
-        drain(out_cov.at[:, c * part:(c + 1) * part], store_sem.at[c])
-    mean_store.wait()
+        drain(part_z.at[:nz - 1, :, :WIDES[c]], rsz_send.at[c])
+        drain(mean_z.at[c, :nz - 1, :, :2 * BLOCK + WIDES[c]], rmz_send.at[c])
+        drain_z(c, agz_send)
+        drain_x(c, agx_send)
 
 
 def body(
@@ -418,46 +426,44 @@
     nx, nz = RING_X, toks // RING_X
     width = patches.shape[1]
     rows = patches.shape[0] // sections
-    part = width // CHUNKS
-    wide = part // nx
+    quarter = width // nx
     slim = BLOCK // nz
-    meta = wide + 2 * BLOCK
+    widest = max(WIDES)
+    meta = widest + 2 * BLOCK
     dma = pltpu.SemaphoreType.DMA
     smem = pl.BlockSpec(memory_space=pltpu.SMEM)
-    hbm = pl.BlockSpec(memory_space=pl.ANY)
+    hbm = pl.BlockSpec(memory_space=pltpu.HBM)
+    on_chip = pl.BlockSpec(memory_space=pltpu.VMEM)
     vmem = pltpu.VMEM
     each = dma((CHUNKS,))
     group = nx * sections * rows
     cov, mean = pl.pallas_call(
         functools.partial(kernel, sections, toks),
         out_shape=(
-            jax.ShapeDtypeStruct((BLOCK, width), BF16),
-            jax.ShapeDtypeStruct((1, width), F32),
+            pltpu.VMEM((nz, slim, width), BF16),
+            pltpu.VMEM((1, width), F32),
         ),
         in_specs=[smem] * 3 + [hbm] * 7,
-        out_specs=(hbm, hbm),
+        out_specs=(on_chip, on_chip),
         scratch_shapes=[
             vmem((rows, width), BF16),
             vmem(pos_table.shape, BF16),
             vmem((2, 1, width), F32),
             vmem((sections, 4, 1, width), F32),
             vmem((rows, width), F32),
-            vmem((sections * nx, rows, BLOCK + CHUNKS * wide), BF16),
-            vmem((nx * sections, rows, BLOCK + CHUNKS * wide), BF16),
+            vmem((sections * nx, rows, BLOCK + quarter), BF16),
+            vmem((nx * sections, rows, BLOCK + quarter), BF16),
             vmem((nx, 1, 128), jnp.int32),
             vmem((16, group), BF16),
             vmem((group, BLOCK), BF16),
             vmem((BLOCK, BLOCK), F32),
             vmem((1, BLOCK), F32),
-            vmem((CHUNKS, nz, slim, wide), BF16),
+            vmem((nz, slim, quarter), BF16),
             vmem((CHUNKS, 1, meta), F32),
-            vmem((CHUNKS, nz, slim, wide), BF16),
+            vmem((nz, slim, quarter), BF16),
             vmem((CHUNKS, nz, 1, meta), F32),
-            vmem((BLOCK, wide), F32),
-            vmem((CHUNKS, BLOCK, wide), BF16),
-            vmem((CHUNKS, nx, BLOCK, wide), BF16),
-            vmem((nx, 1, CHUNKS * wide), F32),
-            vmem((1, width), F32),
+            vmem((BLOCK, widest), F32),
+            vmem((nx, 1, quarter), F32),
             dma((7,)),
             dma((sections // 2,)),
             dma((sections // 2,)),
@@ -470,18 +476,16 @@
             each, each,
             dma((1,)),
             dma((1,)),
-            each,
-            dma((1,)),
         ],
         compiler_params=pltpu.CompilerParams(
-            collective_id=0, has_side_effects=True, vmem_limit_bytes=60 * 1024 * 1024
+            collective_id=0, has_side_effects=True, vmem_limit_bytes=58 * 1024 * 1024
         ),
         name="moments",
     )(
         patch_ids, token_counts, alpha_index, patches, pos_table, norm_gain, norm_bias,
         branch_scale, act_range, weight_range,
     )
-    return cov[None].astype(F32), mean
+    return cov.reshape(1, BLOCK, width).astype(F32), mean
 
 
 def solution(mesh):

time: 73.3 us -> 71.2 us (0.971)
  other arithmetic: 3.4 us -> 1.98 us
    convert_element_type x1, other arithmetic: 3.4 us -> 1.98 us  [body(): return (cov.reshape(1, BLOCK, width).astype(F32), mean)]
where the time goes in v4:
time: 71.2 us; the launch traced here: 71.1 us
  Pallas kernels  66.6 us (94%)
  other arithmetic  1.98 us (3%)
  between operations  1.93 us (3%)
    pallas_call x1, Pallas kernels, body(): pl.pallas_call(functools.partial(kernel, sections, toks), out_shape=(pltp...  66.6 us
    convert_element_type x1, other arithmetic, body(): return (cov.reshape(1, BLOCK, width).astype(F32), mean)  1.98 us

profile of v4, /device:TPU:1, one launch (start us, length us, event | category | flops | bytes accessed | tf_op | source)
XLA Modules:
  0.0 71.1 jit_solution(12320596007977713443)
XLA Ops:
  1.9 66.6 %moments.1 = (bf16[8,16,6144]{2,1,0:T(8,128)(2,1)S(1)}, f32[1,6144]{1,0:T(1,128)S(1)}) custom-call(s32[128]{0:T(128)} %ids.1, s32[1]{0:T(128)S(6)} %copy.14.count, s32[1]{0:T(128)S(6)} %copy.15.alpha, bf16[128,6144]{1,0:T(8,128)(2,1)} %patches.1, bf16[256,6144]{1,0:T(8,128)(2,1)} %table.1, f32[1,6144]{1,0:T(1,128)} %gain.1, f32[1,6144]{1,0:T(1,128)} %bias.1, ...), custom_call_target="tpu_custom_call" | custom-call | tf_op jit(solution)/shard_map/moments/pallas_call | solution.py:440
  68.5 0.6 copy.13
  69.1 2.0 %bitcast_convert_fusion = f32[1,128,6144]{2,1,0:T(8,128)} fusion(bf16[1,128,6144]{2,1,0:T(8,128)(2,1)S(1)} %bitcast.4), kind=kLoop, calls=%fused_computation | loop fusion | flops 786432 | bytes 4718592 | tf_op jit(solution)/shard_map/convert_element_type | solution.py:488

commit v5 on v4

--- a/solution.py
+++ b/solution.py
@@ -12,6 +12,7 @@
 STEP = 768
 UNITS = (3, 3, 3, 3)
 SWAPPED = ()
+RELAY = 3
 WIDES = [128 * n for n in UNITS]
 STARTS = [sum(WIDES[:k]) for k in range(len(WIDES))]
 CHUNKS = len(WIDES)
@@ -73,6 +74,7 @@
     block, block_sum, block_mean, part_z, mean_z_send, gram_z, mean_z, spread, mean_part,
     load_sem, par_send, par_pass, par_recv, cnt_send, cnt_recv, tok_send,
     tok_recv, rsz_send, rsz_recv, rmz_send, rmz_recv, agz_send, agz_recv, agx_send, agx_recv,
+    near_send, near_recv, relay_send, relay_recv,
     agm_send, agm_recv,
 ):
     s = lax.axis_index("section")
@@ -305,6 +307,19 @@
         cols = own_cols(c, x)
         held = final.at[z, :, cols] if c in SWAPPED else final.at[:, :, cols]
         return remote(held, held, agx_send.at[c], agx_recv.at[c], to_x(target))
+
+    def near_copy(c, side):
+        step = 1 if side == 0 else nx - 1
+        held = final.at[:, :, own_cols(c, x)]
+        return remote(held, held, near_send.at[c, side], near_recv.at[c, side],
+                      to_x(lax.rem(x + step, nx)))
+
+    def relay_copy(c, side):
+        step = 1 if side == 0 else nx - 1
+        origin = lax.rem(x + nx - step, nx)
+        held = final.at[pl.ds(side * (nz // 2), nz // 2), :, own_cols(c, origin)]
+        return remote(held, held, relay_send.at[c, side], relay_recv.at[c, side],
+                      to_x(lax.rem(x + step, nx)))
 
     def drain_z(c, sem):
         size = nx * WIDES[c] if c in SWAPPED else WIDES[c]
@@ -381,15 +396,28 @@
             others(nz, z, lambda k: along_z(c, k).start())
         else:
             drain_z(c, agz_recv)
-            others(nx, x, lambda k: along_x(c, k).start())
+            if c < RELAY:
+                near_copy(c, 0).start()
+                near_copy(c, 1).start()
+            else:
+                others(nx, x, lambda k: along_x(c, k).start())
 
     def b_stage(c):
-        if c in SWAPPED:
+        if c < RELAY:
+            for side in range(2):
+                near_copy(c, side).wait_recv()
+                relay_copy(c, side).start()
+        elif c in SWAPPED:
             drain_z(c, agz_recv)
         else:
             drain_x(c, agx_recv)
 
-    stages = (gram_stage, z_stage, a_stage, b_stage)
+    def c_stage(c):
+        if c < RELAY:
+            relay_copy(c, 0).wait_recv()
+            relay_copy(c, 1).wait_recv()
+
+    stages = (gram_stage, z_stage, a_stage, b_stage, c_stage)
     for tick in range(CHUNKS + len(stages) - 1):
         for place, stage in enumerate(stages):
             if 0 <= tick - place < CHUNKS:
@@ -414,7 +442,12 @@
         drain(part_z.at[:nz - 1, :, :WIDES[c]], rsz_send.at[c])
         drain(mean_z.at[c, :nz - 1, :, :2 * BLOCK + WIDES[c]], rmz_send.at[c])
         drain_z(c, agz_send)
-        drain_x(c, agx_send)
+        if c < RELAY:
+            for side in range(2):
+                near_copy(c, side).wait_send()
+                relay_copy(c, side).wait_send()
+        else:
+            drain_x(c, agx_send)
 
 
 def body(
@@ -436,6 +469,7 @@
     on_chip = pl.BlockSpec(memory_space=pltpu.VMEM)
     vmem = pltpu.VMEM
     each = dma((CHUNKS,))
+    pair = dma((CHUNKS, 2))
     group = nx * sections * rows
     cov, mean = pl.pallas_call(
         functools.partial(kernel, sections, toks),
@@ -474,6 +508,7 @@
             each, each, each, each,
             each, each,
             each, each,
+            pair, pair, pair, pair,
             dma((1,)),
             dma((1,)),
         ],

time: 71.2 us -> 70.6 us (level); the launches traced: 71.1 us -> 69.7 us
  Pallas kernels: 66.6 us -> 65.2 us
    pallas_call x1, Pallas kernels: 66.6 us -> 65.2 us  [body(): pl.pallas_call(functools.partial(kernel, sections, toks), out_shape=(pltp...]
where the time goes in v5:
time: 70.6 us; the launch traced here: 69.7 us
  Pallas kernels  65.2 us (92%)
  other arithmetic  1.98 us (3%)
  between operations  1.93 us (3%)
    pallas_call x1, Pallas kernels, body(): pl.pallas_call(functools.partial(kernel, sections, toks), out_shape=(pltp...  65.2 us
    convert_element_type x1, other arithmetic, body(): return (cov.reshape(1, BLOCK, width).astype(F32), mean)  1.98 us

profile of v5, /device:TPU:1, one launch (start us, length us, event | category | flops | bytes accessed | tf_op | source)
XLA Modules:
  0.0 69.7 jit_solution(16723356241144275656)
XLA Ops:
  1.9 65.2 %moments.1 = (bf16[8,16,6144]{2,1,0:T(8,128)(2,1)S(1)}, f32[1,6144]{1,0:T(1,128)S(1)}) custom-call(s32[128]{0:T(128)} %ids.1, s32[1]{0:T(128)S(6)} %copy.14.count, s32[1]{0:T(128)S(6)} %copy.15.alpha, bf16[128,6144]{1,0:T(8,128)(2,1)} %patches.1, bf16[256,6144]{1,0:T(8,128)(2,1)} %table.1, f32[1,6144]{1,0:T(1,128)} %gain.1, f32[1,6144]{1,0:T(1,128)} %bias.1, ...), custom_call_target="tpu_custom_call" | custom-call | tf_op jit(solution)/shard_map/moments/pallas_call | solution.py:474
  67.1 0.6 copy.13
  67.7 2.0 %bitcast_convert_fusion = f32[1,128,6144]{2,1,0:T(8,128)} fusion(bf16[1,128,6144]{2,1,0:T(8,128)(2,1)S(1)} %bitcast.4), kind=kLoop, calls=%fused_computation | loop fusion | flops 786432 | bytes 4718592 | tf_op jit(solution)/shard_map/convert_element_type | solution.py:523
